TPU v7x, 512 devices: a whole 4x8x8 slice. The times are simulated.
512 devices in a mesh: chan: 128 (over x, y_hi, z, core), tblk: 4 (over y_lo).
Axes of the slice: x: 4, y: 8 (y_hi: 2, y_lo: 4; y = y_hi * 4 + y_lo), z: 8, core: 2. Of those that a mesh axis runs over, the one named last changes fastest.
Arguments:
- voltages: bfloat16 [2, 16, 2048, 1024], P(None, 'tblk', 'chan'), may hold values from -6 to 6
- calibrated_gain: float32 [2, 2048, 1024], P(None, 'chan'), may hold values from -4 to 4
- cells: int32 [2, 2048], replicated, may hold values from 0 to 126
- offsets: int32 [2, 2048], replicated, may hold values from 0 to 7
Outputs:
- images: float32 [1024, 128, 128], P(('chan', 'tblk'))
Inputs may be any that keep to these rules, and one draw needn't show every extreme that they name: Each antenna's 2 x 2 footprint of cells lies on the grid.
All inputs are finite; a program needn't handle non-finite values.
Results may differ from a plain program's by a relative error of at most 0.0056.
Values may be sent and summed in bfloat16 or wider, within the bound.
No kernel may reach another device: no remote copies, remote signals or barrier semaphores. Data moves between devices by JAX's collectives and lax.ppermute only.
A program may use at most 128 MiB of HBM per device.

v0:
```python
import math

import jax
import jax.numpy as jnp
from jax import lax
from jax.sharding import PartitionSpec as P

GRID_CELLS = 128
TAPS = 4


def shifted(block, axis, distance):
    devices = range(lax.axis_size(axis))
    route = [(i - distance, i) for i in devices if i - distance in devices]
    return lax.ppermute(block, axis, route)


def dft_table(length):
    points = jnp.arange(length, dtype=jnp.int32)
    product = points[:, None] * points[None, :] % length
    phases = product.astype(jnp.float32) * (2.0 * math.pi / length)
    cosine = jnp.cos(phases)
    sines = jnp.sin(phases)
    real_rows = jnp.stack([cosine, -sines], axis=1)
    imag_rows = jnp.stack([sines, cosine], axis=1)
    return jnp.stack([real_rows, imag_rows], axis=0).astype(jnp.bfloat16)


def prototype(tap_count, channels):
    span_total = tap_count * channels
    places = jnp.arange(span_total, dtype=jnp.int32).astype(jnp.float32) + 0.5
    time_window = 0.54 - 0.46 * jnp.cos(places * (2.0 * math.pi / span_total))
    return (jnp.sinc((places - 0.5 * span_total) / channels) * time_window).reshape(
        tap_count, channels
    )


def twiddle(first_len, second, channels):
    row_points = jnp.arange(first_len, dtype=jnp.int32)
    column_positions = jnp.arange(second, dtype=jnp.int32)
    phases = (row_points[:, None] * column_positions[None, :] % channels).astype(jnp.float32) * (
        2.0 * math.pi / channels
    )
    return (jnp.cos(phases), -jnp.sin(phases))


def channelize(extended, gains, frames):
    tap_count = extended.shape[1] - frames + 1
    antennas = extended.shape[2]
    channels = extended.shape[3]
    second = channels // 32
    filter_taps = prototype(tap_count, channels)
    summed = jnp.zeros((2, frames, antennas, channels), jnp.float32)
    for tap_index in range(tap_count):
        summed = summed + filter_taps[tap_index] * extended[
            :, tap_index : tap_index + frames
        ].astype(jnp.float32)
    windowed = summed.astype(jnp.bfloat16).reshape(2, frames, antennas, 32, second)
    partial_value = jnp.einsum(
        "cfajn,cjdk->dfakn", windowed, dft_table(32), preferred_element_type=jnp.float32
    )
    twist_real, twiddle_imaginary = twiddle(32, second, channels)
    rotated = jnp.stack(
        [
            partial_value[0] * twist_real - partial_value[1] * twiddle_imaginary,
            partial_value[0] * twiddle_imaginary + partial_value[1] * twist_real,
        ]
    ).astype(jnp.bfloat16)
    spectra = jnp.einsum(
        "cfakn,cnem->aefmk", rotated, dft_table(second), preferred_element_type=jnp.float32
    )
    spectra = spectra.reshape(antennas, 2, frames, channels)
    gain_real = gains[0][:, None, :]
    gain_imag = gains[1][:, None, :]
    voltage_out = jnp.stack(
        [
            spectra[:, 0] * gain_real - spectra[:, 1] * gain_imag,
            spectra[:, 0] * gain_imag + spectra[:, 1] * gain_real,
        ],
        axis=1,
    )
    return voltage_out.astype(jnp.bfloat16)


def grid_aperture(volt_block, cells, offsets, grid_size):
    columns = volt_block.shape[2]
    fraction = (offsets.astype(jnp.float32) + 0.5) / 8.0
    row_weight = jnp.stack([1.0 - fraction[0], fraction[0]])
    col_weight = jnp.stack([1.0 - fraction[1], fraction[1]])
    weights = row_weight[:, None, :] * col_weight[None, :, :]
    shifts = jnp.arange(2, dtype=jnp.int32)
    cell_index = (
        (cells[0][None, None, :] + shifts[:, None, None]) * grid_size
        + cells[1][None, None, :]
        + shifts[None, :, None]
    )
    target = jnp.stack([cell_index, cell_index + grid_size * grid_size], axis=-1)
    spread = weights[:, :, :, None, None] * volt_block[None, None].astype(jnp.float32)
    aperture = jax.ops.segment_sum(
        spread.reshape(-1, columns), target.reshape(-1), num_segments=2 * grid_size * grid_size
    )
    return aperture.astype(jnp.bfloat16).reshape(2 * grid_size, grid_size * columns)


def power_block(aperture, grid_size, columns, dft_grid):
    matrix = dft_grid.transpose(2, 3, 0, 1).reshape(2 * grid_size, 2 * grid_size)
    halfway = jnp.dot(matrix, aperture, preferred_element_type=jnp.float32).astype(jnp.bfloat16)
    halfway = halfway.reshape(2, grid_size, grid_size, columns)
    sky_field = jnp.einsum("dkvb,dveh->ekhb", halfway, dft_grid, preferred_element_type=jnp.float32)
    return sky_field[0] * sky_field[0] + sky_field[1] * sky_field[1]


def accumulate(turned, cells, offsets, grid_size):
    antennas = turned.shape[0]
    frames = turned.shape[2]
    channels = turned.shape[3]
    columns = frames * channels
    dft_grid = dft_table(grid_size)
    volt_block = turned.reshape(antennas, 2, columns)
    aperture = grid_aperture(volt_block, cells, offsets, grid_size)
    powers = power_block(aperture, grid_size, columns, dft_grid)
    return powers.reshape(grid_size, grid_size, frames, channels).sum(axis=2)


def local(voltages, calibrated_gain, cells, offsets):
    frames = voltages.shape[1]
    last_frames = voltages[:, frames - (TAPS - 1) :]
    earlier = shifted(last_frames, "tblk", 1)
    extended = jnp.concatenate([earlier, voltages], axis=1)
    voltage_out = channelize(extended, calibrated_gain, frames)
    all_antennas = voltage_out.shape[0] * lax.axis_size("chan")
    all_channels = calibrated_gain.shape[2]
    image_scale = 1.0 / (all_antennas * all_channels * frames * lax.axis_size("tblk"))
    turned = lax.all_to_all(voltage_out, "chan", split_axis=3, concat_axis=0, tiled=True)
    partial_image = jnp.transpose(
        accumulate(turned, cells, offsets, GRID_CELLS) * image_scale, (2, 0, 1)
    )
    return lax.psum_scatter(partial_image, "tblk", scatter_dimension=0, tiled=True)


def solution(mesh):
    placed = (P(None, "tblk", "chan", None), P(None, "chan", None), P(), P())
    return jax.shard_map(
        local,
        mesh=mesh,
        in_specs=placed,
        out_specs=P(("chan", "tblk"), None, None),
        check_vma=False,
    )
```

profile of v0, /device:TPU:1, one launch (start us, length us, event | category | flops | bytes accessed | tf_op | source)
XLA Modules:
  0.0 254.1 jit_solution(14828583791700335229)
XLA Ops:
  7.6 4.0 %collective-permute-start = (bf16[2,3,16,1024]{3,2,1,0:T(8,128)(2,1)S(1)}, bf16[2,3,16,1024]{3,2,1,0:T(8,128)(2,1)S(1)}, u32[]{:S(2)}, u32[]{:S(2)}) collective-permute-start(bf16[2,3,16,1024]{3,2,1,0:T(8,128)(2,1)S(1)} %slice.77), channel_id=1, source_target_pairs={{0,1},{1,2},{2,3},{4,5},{5,6},{6,7},{8,9},{9,10},{10,11},{12,13},{... | collective-permute-start | bytes 589832 | tf_op jit(solution)/shard_map/ppermute | solution.py:15
  19.4 1.4 copy.42
  20.7 3.0 %reshape.318 = bf16[128,2,512]{2,1,0:T(2,128)(2,1)} reshape(bf16[1024,2,4,16]{3,2,1,0:T(4,128)(2,1)S(1)} %bitcast.89) | data formatting | bytes 524288
  23.7 20.5 %all-to-all-start = ((bf16[128,2,512]{2,1,0:T(2,128)(2,1)}), bf16[128,2,512]{2,1,0:T(2,128)(2,1)S(1)}, u32[]{:S(2)}, u32[]{:S(2)}) async-start(bf16[128,2,512]{2,1,0:T(2,128)(2,1)} %reshape.318), calls=%async_computation | async-start | bytes 524288 | tf_op jit(solution)/shard_map/all_to_all | solution.py:134
  44.6 2.6 %mul.541 = f32[2,2,2048,2]{3,2,1,0:T(8,128)} broadcast(f32[2,2,2048]{2,1,0:T(2,128)S(1)} %broadcast_multiply_fusion), dimensions={0,1,2} | broadcast | bytes 98304 | tf_op jit(solution)/shard_map/mul | solution.py:98
  47.1 4.0 %mul.542 = f32[16384]{0:T(1024)S(1)} reshape(f32[2,2,2048,2]{3,2,1,0:T(8,128)} %mul.541) | data formatting | bytes 131072 | tf_op jit(solution)/shard_map/mul | solution.py:98
  51.1 2.6 %copy.38 = s32[2,2,2048,2]{3,2,1,0:T(8,128)} copy(s32[2,2,2048,2]{2,3,1,0:T(2,128)S(1)} %pad_add_fusion) | data formatting | bytes 131072 | tf_op jit(solution)/shard_map/stack | solution.py:97
  53.8 4.0 %reshape.301 = s32[16384]{0:T(1024)S(1)} reshape(s32[2,2,2048,2]{3,2,1,0:T(8,128)} %copy.38) | data formatting | bytes 131072 | tf_op jit(solution)/shard_map/broadcast_in_dim;reshape | solution.py:99
  58.5 1.9 all-to-all-done
  60.5 1.4 reshape.319
  61.9 1.7 copy.43
  63.6 2.3 copy.44
  66.0 4.9 %copy.45 = f32[128,16,2,4,8]{1,0,4,3,2:T(8,128)} copy(f32[128,16,2,4,8]{1,4,0,3,2:T(8,128)} %bitcast.87) | data formatting | bytes 1048576 | tf_op jit(solution)/shard_map/convert_element_type | solution.py:98
  70.9 4.7 %reshape.297 = f32[2048,2,32]{0,2,1:T(8,128)S(1)} reshape(f32[128,16,2,4,8]{1,0,4,3,2:T(8,128)} %copy.45) | data formatting | bytes 1048576 | tf_op jit(solution)/shard_map/convert_element_type | solution.py:98
  76.6 4.1 %mul.592 = f32[2,2,2048,2,32]{4,3,2,1,0:T(2,128)} broadcast(f32[2048,2,32]{2,1,0:T(2,128)S(1)} %copy.46), dimensions={2,3,4} | broadcast | bytes 2621440 | tf_op jit(solution)/shard_map/mul | solution.py:98
  80.8 102.8 %scatter_custom_fusion = f32[32768,32]{1,0:T(8,128)} fusion(s32[16384]{0:T(1024)S(1)} %reshape.301, f32[16384,32]{1,0:T(8,128)} %bitcast.86, f32[]{:T(128)} %constant.89.clone.1, f32[16384]{0:T(1024)S(1)} %mul.542), kind=kCustom, calls=%fused_computation.1 | custom fusion | flops 1048576 | bytes 6356996 | tf_op jit(solution)/shard_map/scatter-add | solution.py:99
  183.6 8.9 %convert_element_type.139 = bf16[32768,32]{1,0:T(8,128)(2,1)} convert(f32[32768,32]{1,0:T(8,128)} %scatter_custom_fusion) | non-fusion elementwise | flops 1048576 | bytes 6291456 | tf_op jit(solution)/shard_map/convert_element_type | solution.py:102
  192.5 10.7 %reshape.295 = bf16[256,4096]{1,0:T(8,128)(2,1)S(1)} reshape(bf16[32768,32]{1,0:T(8,128)(2,1)} %convert_element_type.139) | data formatting | bytes 4194304 | tf_op jit(solution)/shard_map/reshape | solution.py:102
  203.1 2.0 convolution_convert_fusion
  205.2 3.3 %copy.47 = bf16[256,4096]{0,1:T(8,128)(2,1)S(1)} copy(bf16[256,4096]{1,0:T(8,128)(2,1)} %convolution_convert_fusion) | data formatting | bytes 4194304 | tf_op jit(solution)/shard_map/convert_element_type | solution.py:107
  208.5 2.1 reshape.296
  210.5 5.0 %copy.48 = bf16[2,128,128,32]{2,1,0,3:T(8,128)(2,1)S(1)} copy(bf16[2,128,128,32]{1,0,3,2:T(2,128)(2,1)} %reshape.296) | data formatting | bytes 4194304 | tf_op jit(solution)/shard_map/reshape | solution.py:108
  217.6 28.0 %reduce-scatter.2.cloned.1.call-done = f32[2,128,128]{1,2,0:T(8,128)} async-done(((f32[8,128,128]{1,2,0:T(8,128)}), f32[2,128,128]{1,2,0:T(8,128)}) %reduce-scatter.2.cloned.1.call-update) | async-done | bytes 131088 | tf_op jit(solution)/shard_map/reduce_scatter | solution.py:138
  245.6 1.7 copy.49
  (41 shorter events, 12.7 us)
Async XLA Ops:
  6.5 9.1 %copy-start = (bf16[2,4,16,1024]{3,2,1,0:T(8,128)(2,1)S(1)}, bf16[2,4,16,1024]{3,2,1,0:T(8,128)(2,1)}, u32[]{:S(2)}) copy-start(bf16[2,4,16,1024]{3,2,1,0:T(8,128)(2,1)} %param.4) | copy-start | bytes 786436
  7.6 7.1 %collective-permute-start = (bf16[2,3,16,1024]{3,2,1,0:T(8,128)(2,1)S(1)}, bf16[2,3,16,1024]{3,2,1,0:T(8,128)(2,1)S(1)}, u32[]{:S(2)}, u32[]{:S(2)}) collective-permute-start(bf16[2,3,16,1024]{3,2,1,0:T(8,128)(2,1)S(1)} %slice.77), channel_id=1, source_target_pairs={{0,1},{1,2},{2,3},{4,5},{5,6},{6,7},{8,9},{9,10},{10,11},{12,13},{... | collective-permute-start | bytes 589832 | tf_op jit(solution)/shard_map/ppermute | solution.py:15
  23.7 36.8 %all-to-all-start = ((bf16[128,2,512]{2,1,0:T(2,128)(2,1)}), bf16[128,2,512]{2,1,0:T(2,128)(2,1)S(1)}, u32[]{:S(2)}, u32[]{:S(2)}) async-start(bf16[128,2,512]{2,1,0:T(2,128)(2,1)} %reshape.318), calls=%async_computation | async-start | bytes 524288 | tf_op jit(solution)/shard_map/all_to_all | solution.py:134
  44.3 201.4 %reduce-scatter.2.cloned.1.call-start = ((), (), s32[]{:S(2)}) async-start(), calls=%async_computation.2 | async-start | bytes 655360 | tf_op jit(solution)/shard_map/reduce_scatter | solution.py:138
Sparse Core Ops, SparseCore 0:
  217.7 27.8 reduce-scatter.1
where the time goes:
time: 256 us; the launch traced here: 254 us
  other arithmetic  115 us (45%)
  local copies, waits for them, and re-layouts  66 us (26%)
  waiting for transfers between devices  30 us (12%)
  starting transfers between devices  24.8 us (10%)
  between operations  13.7 us (5%)
  matrix products  4.23 us (2%)
    scatter-add x1, other arithmetic, grid_aperture(): jax.ops.segment_sum(spread.reshape(-1, columns), target.reshape(-1), num_...  103 us
    reduce_scatter x1, waiting for transfers between devices, local(): lax.psum_scatter(partial_image, 'tblk', scatter_dimension=0, tiled=True)  28 us
    all_to_all x1, starting transfers between devices, local(): lax.all_to_all(voltage_out, 'chan', split_axis=3, concat_axis=0, tiled=True)  20.5 us
    convert_element_type x4, local copies, waits for them, and re-layouts, grid_aperture(): volt_block[None, None].astype(jnp.float32)  13 us
    mul x3, local copies, waits for them, and re-layouts, grid_aperture(): weights[:, :, :, None, None] * volt_block[None, None].astype(jnp.float32)  10.7 us
    reshape x1, local copies, waits for them, and re-layouts, grid_aperture(): aperture.astype(jnp.bfloat16).reshape(2 * grid_size, grid_size * columns)  10.7 us
    convert_element_type x1, other arithmetic, grid_aperture(): aperture.astype(jnp.bfloat16).reshape(2 * grid_size, grid_size * columns)  8.89 us
    reshape x2, local copies, waits for them, and re-layouts, power_block(): halfway = halfway.reshape(2, grid_size, grid_size, columns)  7.03 us
  transfers between devices with their start and end apart: 3, of which 2 were waited for; matrix products, arithmetic and copies ran while one was open for 7% of the time, Pallas kernels for 0%

commit v1 on v0

v1 whole, which is shorter than its diff:
```python
import math

import jax
import jax.numpy as jnp
import numpy as np
from jax import lax
from jax.experimental import pallas as pl
from jax.experimental.pallas import tpu as pltpu
from jax.sharding import PartitionSpec as P

GRID = 128
TAPS = 4
FIRST = 8
HALF = GRID // 2
VMEM_BYTES = 48 * 1024 * 1024


def prototype(channels):
    span = TAPS * channels
    places = np.arange(span, dtype=np.float64) + 0.5
    window = 0.54 - 0.46 * np.cos(places * (2.0 * math.pi / span))
    return (np.sinc((places - 0.5 * span) / channels) * window).reshape(TAPS, channels).astype(np.float32)


def twiddle(channels):
    second = channels // FIRST
    phases = (np.arange(FIRST)[:, None] * np.arange(second)[None, :] % channels) * (2.0 * math.pi / channels)
    return np.stack([np.cos(phases), -np.sin(phases)]).astype(np.float32)


def dft_parts(length):
    points = np.arange(length)
    phases = (points[:, None] * points[None, :] % length) * (2.0 * math.pi / length)
    return np.cos(phases), np.sin(phases)


def dft_right(length):
    cosine, sine = dft_parts(length)
    return np.block([[cosine, -sine], [sine, cosine]]).astype(jnp.bfloat16)


def dft_left(length):
    cosine, sine = dft_parts(length)
    return np.block([[cosine, sine], [-sine, cosine]]).astype(jnp.bfloat16)


def eight_points(re, im):
    add = lambda p, q: (p[0] + q[0], p[1] + q[1])
    sub = lambda p, q: (p[0] - q[0], p[1] - q[1])
    sub_i = lambda p, q: (p[0] + q[1], p[1] - q[0])
    add_i = lambda p, q: (p[0] - q[1], p[1] + q[0])
    root = math.sqrt(0.5)
    w = list(zip(re, im))
    a0, a1, a2, a3 = add(w[0], w[4]), sub(w[0], w[4]), add(w[2], w[6]), sub(w[2], w[6])
    a4, a5, a6, a7 = add(w[1], w[5]), sub(w[1], w[5]), add(w[3], w[7]), sub(w[3], w[7])
    b0, b2, b1, b3 = add(a0, a2), sub(a0, a2), sub_i(a1, a3), add_i(a1, a3)
    b4, b6, b5, b7 = add(a4, a6), sub(a4, a6), sub_i(a5, a7), add_i(a5, a7)
    c5 = ((b5[0] + b5[1]) * root, (b5[1] - b5[0]) * root)
    c7 = ((b7[1] - b7[0]) * root, (b7[0] + b7[1]) * -root)
    return [
        add(b0, b4), add(b1, c5), sub_i(b2, b6), add(b3, c7),
        sub(b0, b4), sub(b1, c5), add_i(b2, b6), sub(b3, c7),
    ]


def channelize_kernel(frames, volt_ref, gain_ref, taps_ref, twist_ref, table_ref, out_ref,
                      part_ref, turn_ref, sorted_ref):
    antennas = volt_ref.shape[2]
    channels = volt_ref.shape[3]
    second = channels // FIRST
    spans = frames + TAPS - 1
    both = jnp.concatenate([gain_ref[0], gain_ref[1]], axis=0)
    turn_ref[:, 0 : 2 * antennas] = both.T
    for g in range(spans):
        values = []
        for c in range(2):
            total = None
            for p in range(TAPS):
                f = g - (TAPS - 1) + p
                if 0 <= f < frames:
                    term = volt_ref[c, f].astype(jnp.float32) * taps_ref[p : p + 1, :]
                    total = term if total is None else total + term
            total = total.astype(jnp.bfloat16).astype(jnp.float32)
            values.append([total[:, j * second : (j + 1) * second] for j in range(FIRST)])
        for k, (re, im) in enumerate(eight_points(*values)):
            tw_re = twist_ref[0, k : k + 1, :]
            tw_im = twist_ref[1, k : k + 1, :]
            if k == 0:
                out_re, out_im = re, im
            else:
                out_re = re * tw_re - im * tw_im
                out_im = re * tw_im + im * tw_re
            part_ref[k, g * antennas : (g + 1) * antennas, 0:second] = out_re.astype(jnp.bfloat16)
            part_ref[k, g * antennas : (g + 1) * antennas, second:] = out_im.astype(jnp.bfloat16)
    blank = jnp.zeros(((2 * frames - spans) * antennas, second), jnp.float32)
    for k in range(FIRST):
        spectra = jnp.dot(part_ref[k], table_ref[...], preferred_element_type=jnp.float32)
        gains = turn_ref[pl.ds(k, second, stride=FIRST), 0 : 2 * antennas].T
        gain_re = jnp.concatenate([gains[0:antennas]] * spans, axis=0)
        gain_im = jnp.concatenate([gains[antennas:]] * spans, axis=0)
        re, im = spectra[:, 0:second], spectra[:, second:]
        for c, volts in enumerate((re * gain_re - im * gain_im, re * gain_im + im * gain_re)):
            turned = jnp.concatenate([volts, blank], axis=0).T
            sorted_ref[pl.ds(2 * k + c, second, stride=2 * FIRST), :] = turned
    out_ref[...] = sorted_ref[...].astype(jnp.bfloat16)


def footprint_kernel(cells_ref, offsets_ref, right_ref, left_ref):
    count = cells_ref.shape[1]
    rows, cols = cells_ref[0:1, :], cells_ref[1:2, :]
    share = (offsets_ref[...].astype(jnp.float32) + 0.5) * 0.125
    t_row, t_col = share[0:1, :], share[1:2, :]
    upper = (rows >= HALF).astype(jnp.int32)
    low = rows - upper * HALF
    place = upper * GRID + cols

    def table(height, first, weight):
        at = lax.broadcasted_iota(jnp.int32, (height, count), 0)
        near = jnp.where(at == first, 1.0 - weight, 0.0)
        return jnp.where(at == first + 1, weight, near).astype(jnp.bfloat16)

    right_ref[...] = table(2 * GRID, place, t_col)
    left_ref[...] = table(left_ref.shape[0], low, t_row)


def image_kernel(scale, x_ref, right_ref, left_ref, first_ref, second_ref, out_ref,
                 wide_ref, volt_ref, spread_ref, grid_ref, side_ref, mid_ref):
    blocks = 4
    frames = 4
    antennas = 16
    step = 4 * blocks
    wide_ref[...] = x_ref[...].astype(jnp.float32)
    for kk in range(2):
        for c in range(2):
            tail = None
            for t in range(blocks):
                turned = wide_ref[pl.ds(4 * t + 2 * kk + c, 128, stride=step), :].T
                own = turned[0 : frames * antennas]
                if tail is not None:
                    own = jnp.concatenate(
                        [own[0 : (TAPS - 1) * antennas] + tail, own[(TAPS - 1) * antennas :]], axis=0)
                tail = turned[frames * antennas : (frames + TAPS - 1) * antennas]
                for f in range(frames):
                    volt_ref[kk * blocks + t, 2 * f + c] = own[f * antennas : (f + 1) * antennas]

    out_ref[...] = jnp.zeros_like(out_ref)
    members = 2 * frames

    def chunk(i, carry):
        for a in range(antennas):
            lanes = slice(a * 128, (a + 1) * 128)
            left = left_ref[0:HALF, lanes]
            for m in range(members):
                row = volt_ref[i, m, a : a + 1, :].astype(jnp.bfloat16)
                spread_ref[m * HALF : (m + 1) * HALF, lanes] = left * row
            edge = volt_ref[i, :, a, :]
            edge = jnp.concatenate([edge, edge], axis=0).astype(jnp.bfloat16)
            spread_ref[members * HALF :, lanes] = edge * left_ref[HALF : HALF + 1, lanes]
        grid_ref[...] = lax.dot_general(
            spread_ref[...], right_ref[...], (((1,), (1,)), ((), ())),
            preferred_element_type=jnp.float32)
        for m in range(members):
            grid_ref[m * HALF : m * HALF + 1, GRID:] += grid_ref[
                members * HALF + m : members * HALF + m + 1, 0:GRID]
        for f in range(frames):
            for c in range(2):
                m = 2 * f + c
                for h in range(2):
                    side_ref[f * GRID + h * HALF : f * GRID + (h + 1) * HALF, c * GRID : (c + 1) * GRID] = grid_ref[
                        m * HALF : (m + 1) * HALF, h * GRID : (h + 1) * GRID].astype(jnp.bfloat16)
        half = jnp.dot(side_ref[...], first_ref[...], preferred_element_type=jnp.float32).astype(jnp.bfloat16)
        for f in range(frames):
            for c in range(2):
                mid_ref[c * GRID : (c + 1) * GRID, f * GRID : (f + 1) * GRID] = half[
                    f * GRID : (f + 1) * GRID, c * GRID : (c + 1) * GRID]
        sky = jnp.dot(second_ref[...], mid_ref[...], preferred_element_type=jnp.float32)
        power = sky[0:GRID] * sky[0:GRID] + sky[GRID:] * sky[GRID:]
        total = power[:, 0:GRID]
        for f in range(1, frames):
            total = total + power[:, f * GRID : (f + 1) * GRID]
        out_ref[i // blocks] += total * scale
        return carry

    lax.fori_loop(0, 2 * blocks, chunk, 0)


def whole(shape):
    return pl.BlockSpec(shape, lambda: (0,) * len(shape))


def local(voltages, calibrated_gain, cells, offsets):
    _, frames, antennas, channels = voltages.shape
    second = channels // FIRST
    devices = lax.axis_size("chan") * lax.axis_size("tblk")
    all_antennas = antennas * lax.axis_size("chan")
    scale = 1.0 / (all_antennas * channels * frames * lax.axis_size("tblk"))
    rows = channels * 2

    send = pl.pallas_call(
        lambda *refs: channelize_kernel(frames, *refs),
        out_shape=jax.ShapeDtypeStruct((rows, second), jnp.bfloat16),
        scratch_shapes=[
            pltpu.VMEM((FIRST, (frames + TAPS - 1) * antennas, 2 * second), jnp.bfloat16),
            pltpu.VMEM((channels, 128), jnp.float32),
            pltpu.VMEM((rows, second), jnp.float32),
        ],
        compiler_params=pltpu.CompilerParams(vmem_limit_bytes=VMEM_BYTES),
        name="channelize",
    )(
        voltages, calibrated_gain, jnp.asarray(prototype(channels)),
        jnp.asarray(twiddle(channels)), jnp.asarray(dft_right(second)),
    )

    def by_member(table):
        return table.reshape(2, all_antennas // antennas, antennas).transpose(0, 2, 1).reshape(2, all_antennas)

    right, left = pl.pallas_call(
        footprint_kernel,
        out_shape=(
            jax.ShapeDtypeStruct((2 * GRID, all_antennas), jnp.bfloat16),
            jax.ShapeDtypeStruct((HALF + 16, all_antennas), jnp.bfloat16),
        ),
        compiler_params=pltpu.CompilerParams(vmem_limit_bytes=VMEM_BYTES),
        cost_estimate=pl.CostEstimate(flops=10_000_000, bytes_accessed=1_500_000, transcendentals=0),
        name="footprint",
    )(by_member(cells), by_member(offsets))

    send = send.reshape(devices, rows // devices, second)
    received = lax.all_to_all(send, ("chan", "tblk"), split_axis=0, concat_axis=0, tiled=True)
    received = received.reshape(rows, second)

    members = 2 * frames
    return pl.pallas_call(
        lambda *refs: image_kernel(scale, *refs),
        out_shape=jax.ShapeDtypeStruct((2, GRID, GRID), jnp.float32),
        scratch_shapes=[
            pltpu.VMEM((rows, second), jnp.float32),
            pltpu.VMEM((8, members, antennas, 128), jnp.float32),
            pltpu.VMEM((members * HALF + 16, all_antennas), jnp.bfloat16),
            pltpu.VMEM((members * HALF + 16, 2 * GRID), jnp.float32),
            pltpu.VMEM((frames * GRID, 2 * GRID), jnp.bfloat16),
            pltpu.VMEM((2 * GRID, frames * GRID), jnp.bfloat16),
        ],
        compiler_params=pltpu.CompilerParams(vmem_limit_bytes=VMEM_BYTES),
        name="image",
    )(received, right, left, jnp.asarray(dft_right(GRID)), jnp.asarray(dft_left(GRID)))


def solution(mesh):
    placed = (P(None, "tblk", "chan", None), P(None, "chan", None), P(), P())
    return jax.shard_map(
        local,
        mesh=mesh,
        in_specs=placed,
        out_specs=P(("chan", "tblk"), None, None),
        check_vma=False,
    )
```

time: 256 us -> 63 us (0.25)
  other arithmetic: 115 us -> 0 us
  local copies, waits for them, and re-layouts: 66 us -> 5.19 us
  Pallas kernels: 0 us -> 15.1 us
  between operations: 13.7 us -> 0.08 us
  waiting for transfers between devices: 30 us -> 20 us
  matrix products: 4.23 us -> 0 us
  starting transfers between devices: 24.8 us -> 22.2 us
    scatter-add x1 -> x0, other arithmetic: 103 us -> none  [grid_aperture(): jax.ops.segment_sum(spread.reshape(-1, columns), target.reshape(-1), num_...]
    reduce_scatter x1 -> x0, waiting for transfers between devices: 28 us -> none  [local(): lax.psum_scatter(partial_image, 'tblk', scatter_dimension=0, tiled=True)]
    reshape x5 -> x3, local copies, waits for them, and re-layouts: 19.4 us -> 0.23 us  [by_member(): table.reshape(2, all_antennas // antennas, antennas).transpose(0, 2, 1)]
    all_to_all x1, waiting for transfers between devices: 1.94 us -> 20 us  [local(): lax.all_to_all(send, ('chan', 'tblk'), split_axis=0, concat_axis=0, tiled...]
    convert_element_type x5 -> x0, local copies, waits for them, and re-layouts: 16.2 us -> none  [the longest x4 13 us: grid_aperture(): volt_block[None, None].astype(jnp.float32)]
    pallas_call x0 -> x3, Pallas kernels: none -> 15.1 us  [the longest x1 12.4 us: local(): pl.pallas_call(lambda *refs: image_kernel(scale, *refs), out_shape=jax.Sh...]
    mul x4 -> x0, local copies, waits for them, and re-layouts: 11.6 us -> none  [the longest x3 10.7 us: grid_aperture(): weights[:, :, :, None, None] * volt_block[None, None].astype(jnp.float32)]
    convert_element_type x2 -> x0, other arithmetic: 9.07 us -> none  [the longest x1 8.89 us: grid_aperture(): aperture.astype(jnp.bfloat16).reshape(2 * grid_size, grid_size * columns)]
  transfers between devices with their start and end apart: 3 -> 1, of which waited for: 2 -> 1; matrix products, arithmetic and copies ran while one was open for 7% -> 1% of each run, Pallas kernels for 0% -> 1%
where the time goes in v1:
time: 63 us; the launch traced here: 62.6 us
  starting transfers between devices  22.2 us (35%)
  waiting for transfers between devices  20 us (32%)
  Pallas kernels  15.1 us (24%)
  local copies, waits for them, and re-layouts  5.19 us (8%)
    all_to_all x1, starting transfers between devices, local(): lax.all_to_all(send, ('chan', 'tblk'), split_axis=0, concat_axis=0, tiled...  22.2 us
    all_to_all x1, waiting for transfers between devices, local(): lax.all_to_all(send, ('chan', 'tblk'), split_axis=0, concat_axis=0, tiled...  20 us
    pallas_call x1, Pallas kernels, local(): pl.pallas_call(lambda *refs: image_kernel(scale, *refs), out_shape=jax.Sh...  12.4 us
    unnamed x18, local copies, waits for them, and re-layouts  4.84 us
    pallas_call x1, Pallas kernels, local(): pl.pallas_call(lambda *refs: channelize_kernel(frames, *refs), out_shape=...  2.11 us
  transfers between devices with their start and end apart: 1, of which 1 were waited for; matrix products, arithmetic and copies ran while one was open for 1% of the time, Pallas kernels for 1%

profile of v1, /device:TPU:1, one launch (start us, length us, event | category | flops | bytes accessed | tf_op | source)
XLA Modules:
  0.0 62.6 jit_solution(14066147608929547953)
XLA Ops:
  0.0 0.0 copy-start
  0.0 0.9 %copy-done = bf16[256,256]{1,0:T(8,128)(2,1)S(1)} copy-done((bf16[256,256]{1,0:T(8,128)(2,1)S(1)}, bf16[256,256]{1,0:T(8,128)(2,1)}, u32[]{:S(2)}) %copy-start) | copy-done | bytes 131096
  0.9 0.0 copy-start.2
  0.9 0.9 %copy-done.2 = bf16[2,4,16,1024]{3,2,1,0:T(8,128)(2,1)S(1)} copy-done((bf16[2,4,16,1024]{3,2,1,0:T(8,128)(2,1)S(1)}, bf16[2,4,16,1024]{3,2,1,0:T(8,128)(2,1)}, u32[]{:S(2)}) %copy-start.2) | copy-done | bytes 262168
  1.9 0.0 copy-start.4
  1.9 0.9 %copy-done.4 = f32[2,16,1024]{2,1,0:T(8,128)S(1)} copy-done((f32[2,16,1024]{2,1,0:T(8,128)S(1)}, f32[2,16,1024]{2,1,0:T(8,128)}, u32[]{:S(2)}) %copy-start.4) | copy-done | bytes 131096
  2.8 0.7 %copy-done.5 = f32[4,1024]{1,0:T(4,128)S(1)} copy-done((f32[4,1024]{1,0:T(4,128)S(1)}, f32[4,1024]{1,0:T(4,128)}, u32[]{:S(2)}) %copy-start.5) | copy-done | bytes 16408
  3.5 0.7 %copy-done.6 = f32[2,8,128]{2,1,0:T(8,128)S(1)} copy-done((f32[2,8,128]{2,1,0:T(8,128)S(1)}, f32[2,8,128]{2,1,0:T(8,128)}, u32[]{:S(2)}) %copy-start.6) | copy-done | bytes 8216
  4.2 2.1 %channelize.1 = bf16[2048,128]{1,0:T(8,128)(2,1)} custom-call(bf16[2,4,16,1024]{3,2,1,0:T(8,128)(2,1)S(1)} %copy-done.2, f32[2,16,1024]{2,1,0:T(8,128)S(1)} %copy-done.4, f32[4,1024]{1,0:T(4,128)S(1)} %copy-done.5, f32[2,8,128]{2,1,0:T(8,128)S(1)} %copy-done.6, bf16[256,256]{1,0:T(8,128)(2,1)S(1)} %copy-done), custom_call_target="tpu_custom_call" | custom-call | tf_op jit(solution)/shard_map/channelize/pallas_call | solution.py:199
  6.3 22.2 %all-to-all-start = ((bf16[512,4,128]{2,1,0:T(4,128)(2,1)}), bf16[512,4,128]{2,1,0:T(4,128)(2,1)S(1)}, u32[]{:S(2)}, u32[]{:S(2)}) async-start(bf16[512,4,128]{2,1,0:T(4,128)(2,1)} %bitcast), calls=%async_computation | async-start | bytes 1048576 | tf_op jit(solution)/shard_map/all_to_all | solution.py:229
  28.5 0.0 copy-done.7
  28.5 0.1 reshape.20
  28.6 0.0 copy-start.8
  28.6 0.1 copy.12
  28.6 0.6 %copy-done.8 = s32[2,2048]{1,0:T(2,128)S(1)} copy-done((s32[2,2048]{1,0:T(2,128)S(1)}, s32[2,2048]{1,0:T(2,128)}, u32[]{:S(2)}) %copy-start.8) | copy-done | bytes 16408
  29.3 0.1 reshape.22
  29.4 0.0 copy-start.1
  29.4 0.0 copy-start.3
  29.4 0.1 copy.13
  29.5 0.6 footprint.1
  30.1 20.0 %all-to-all-done = bf16[512,4,128]{2,1,0:T(4,128)(2,1)S(1)} async-done(((bf16[512,4,128]{2,1,0:T(4,128)(2,1)}), bf16[512,4,128]{2,1,0:T(4,128)(2,1)S(1)}, u32[]{:S(2)}, u32[]{:S(2)}) %all-to-all-start) | async-done | bytes 524320 | tf_op jit(solution)/shard_map/all_to_all | solution.py:229
  50.2 0.0 copy-done.1
  50.2 0.0 copy-done.3
  50.2 12.4 %image.1 = f32[2,128,128]{2,1,0:T(8,128)} custom-call(bf16[2048,128]{1,0:T(8,128)(2,1)S(1)} %bitcast.10, bf16[256,2048]{1,0:T(8,128)(2,1)S(1)} %get-tuple-element.7.refs_1_, bf16[80,2048]{1,0:T(8,128)(2,1)S(1)} %get-tuple-element.8.refs_2_, bf16[256,256]{1,0:T(8,128)(2,1)S(1)} %copy-done.1, bf16[256,256]{1,0:T(8,128)(2,1)S(1)} %copy-done.3), custom_call_target="tpu_custom_call" | custom-call | tf_op jit(solution)/shard_map/image/pallas_call | solution.py:233
  (4 shorter events, 0.0 us)
Async XLA Ops:
  0.0 0.9 %copy-start = (bf16[256,256]{1,0:T(8,128)(2,1)S(1)}, bf16[256,256]{1,0:T(8,128)(2,1)}, u32[]{:S(2)}) copy-start(bf16[256,256]{1,0:T(8,128)(2,1)} %constant.10.clone.refs_4_.refs_3_) | copy-start | bytes 393220
  0.9 0.9 %copy-start.2 = (bf16[2,4,16,1024]{3,2,1,0:T(8,128)(2,1)S(1)}, bf16[2,4,16,1024]{3,2,1,0:T(8,128)(2,1)}, u32[]{:S(2)}) copy-start(bf16[2,4,16,1024]{3,2,1,0:T(8,128)(2,1)} %refs_0_.1) | copy-start | bytes 786436
  1.9 0.9 %copy-start.4 = (f32[2,16,1024]{2,1,0:T(8,128)S(1)}, f32[2,16,1024]{2,1,0:T(8,128)}, u32[]{:S(2)}) copy-start(f32[2,16,1024]{2,1,0:T(8,128)} %refs_1_.1) | copy-start | bytes 393220
  2.8 0.7 %copy-start.5 = (f32[4,1024]{1,0:T(4,128)S(1)}, f32[4,1024]{1,0:T(4,128)}, u32[]{:S(2)}) copy-start(f32[4,1024]{1,0:T(4,128)} %constant.8.clone.refs_2_) | copy-start | bytes 49156
  3.5 0.7 %copy-start.6 = (f32[2,8,128]{2,1,0:T(8,128)S(1)}, f32[2,8,128]{2,1,0:T(8,128)}, u32[]{:S(2)}) copy-start(f32[2,8,128]{2,1,0:T(8,128)} %constant.9.clone.refs_3_) | copy-start | bytes 24580
  6.3 22.2 %copy-start.7 = (s32[2,2048]{1,0:T(2,128)S(1)}, s32[2,2048]{1,0:T(2,128)}, u32[]{:S(2)}) copy-start(s32[2,2048]{1,0:T(2,128)} %param.11) | copy-start | bytes 49156
  6.3 43.9 %all-to-all-start = ((bf16[512,4,128]{2,1,0:T(4,128)(2,1)}), bf16[512,4,128]{2,1,0:T(4,128)(2,1)S(1)}, u32[]{:S(2)}, u32[]{:S(2)}) async-start(bf16[512,4,128]{2,1,0:T(4,128)(2,1)} %bitcast), calls=%async_computation | async-start | bytes 1048576 | tf_op jit(solution)/shard_map/all_to_all | solution.py:229
  28.6 0.7 %copy-start.8 = (s32[2,2048]{1,0:T(2,128)S(1)}, s32[2,2048]{1,0:T(2,128)}, u32[]{:S(2)}) copy-start(s32[2,2048]{1,0:T(2,128)} %param.12) | copy-start | bytes 49156
  29.4 20.8 %copy-start.1 = (bf16[256,256]{1,0:T(8,128)(2,1)S(1)}, bf16[256,256]{1,0:T(8,128)(2,1)}, u32[]{:S(2)}) copy-start(bf16[256,256]{1,0:T(8,128)(2,1)} %constant.10.clone.refs_4_.refs_3_) | copy-start | bytes 393220
  29.4 20.7 %copy-start.3 = (bf16[256,256]{1,0:T(8,128)(2,1)S(1)}, bf16[256,256]{1,0:T(8,128)(2,1)}, u32[]{:S(2)}) copy-start(bf16[256,256]{1,0:T(8,128)(2,1)} %constant.11.clone.refs_4_) | copy-start | bytes 393220

commit v2 on v1

--- a/solution.py
+++ b/solution.py
@@ -12,7 +12,8 @@
 TAPS = 4
 FIRST = 8
 HALF = GRID // 2
-VMEM_BYTES = 48 * 1024 * 1024
+CHUNK = 8
+VMEM_BYTES = 32 * 1024 * 1024
 
 
 def prototype(channels):
@@ -63,14 +64,20 @@
     ]
 
 
-def channelize_kernel(frames, volt_ref, gain_ref, taps_ref, twist_ref, table_ref, out_ref,
-                      part_ref, turn_ref, sorted_ref):
+def channelize_kernel(frames, volt_hbm, gain_hbm, taps_hbm, twist_hbm, table_hbm, out_ref,
+                      volt_ref, gain_ref, taps_ref, twist_ref, table_ref,
+                      part_ref, turn_ref, sorted_ref, sems):
+    sources = (volt_hbm, taps_hbm, twist_hbm, gain_hbm, table_hbm)
+    targets = (volt_ref, taps_ref, twist_ref, gain_ref, table_ref)
+    copies = [pltpu.make_async_copy(s, t, sems.at[i]) for i, (s, t) in enumerate(zip(sources, targets))]
+    for copy in copies:
+        copy.start()
     antennas = volt_ref.shape[2]
     channels = volt_ref.shape[3]
     second = channels // FIRST
     spans = frames + TAPS - 1
-    both = jnp.concatenate([gain_ref[0], gain_ref[1]], axis=0)
-    turn_ref[:, 0 : 2 * antennas] = both.T
+    for copy in copies[0:3]:
+        copy.wait()
     for g in range(spans):
         values = []
         for c in range(2):
@@ -90,11 +97,17 @@
             else:
                 out_re = re * tw_re - im * tw_im
                 out_im = re * tw_im + im * tw_re
-            part_ref[k, g * antennas : (g + 1) * antennas, 0:second] = out_re.astype(jnp.bfloat16)
-            part_ref[k, g * antennas : (g + 1) * antennas, second:] = out_im.astype(jnp.bfloat16)
+            row = (k * spans + g) * antennas
+            part_ref[row : row + antennas, 0:second] = out_re.astype(jnp.bfloat16)
+            part_ref[row : row + antennas, second:] = out_im.astype(jnp.bfloat16)
+    copies[3].wait()
+    both = jnp.concatenate([gain_ref[0], gain_ref[1]], axis=0)
+    turn_ref[:, 0 : 2 * antennas] = both.T
+    copies[4].wait()
     blank = jnp.zeros(((2 * frames - spans) * antennas, second), jnp.float32)
+    all_spectra = jnp.dot(part_ref[...], table_ref[...], preferred_element_type=jnp.float32)
     for k in range(FIRST):
-        spectra = jnp.dot(part_ref[k], table_ref[...], preferred_element_type=jnp.float32)
+        spectra = all_spectra[k * spans * antennas : (k + 1) * spans * antennas]
         gains = turn_ref[pl.ds(k, second, stride=FIRST), 0 : 2 * antennas].T
         gain_re = jnp.concatenate([gains[0:antennas]] * spans, axis=0)
         gain_im = jnp.concatenate([gains[antennas:]] * spans, axis=0)
@@ -124,7 +137,7 @@
 
 
 def image_kernel(scale, x_ref, right_ref, left_ref, first_ref, second_ref, out_ref,
-                 wide_ref, volt_ref, spread_ref, grid_ref, side_ref, mid_ref):
+                 wide_ref, volt_ref, spread_ref, grid_ref, side_ref):
     blocks = 4
     frames = 4
     antennas = 16
@@ -141,10 +154,10 @@
                         [own[0 : (TAPS - 1) * antennas] + tail, own[(TAPS - 1) * antennas :]], axis=0)
                 tail = turned[frames * antennas : (frames + TAPS - 1) * antennas]
                 for f in range(frames):
-                    volt_ref[kk * blocks + t, 2 * f + c] = own[f * antennas : (f + 1) * antennas]
-
-    out_ref[...] = jnp.zeros_like(out_ref)
-    members = 2 * frames
+                    row = (kk * blocks + t) * frames + f
+                    volt_ref[row // CHUNK, 2 * (row % CHUNK) + c] = own[f * antennas : (f + 1) * antennas]
+
+    members = 2 * CHUNK
 
     def chunk(i, carry):
         for a in range(antennas):
@@ -153,8 +166,7 @@
             for m in range(members):
                 row = volt_ref[i, m, a : a + 1, :].astype(jnp.bfloat16)
                 spread_ref[m * HALF : (m + 1) * HALF, lanes] = left * row
-            edge = volt_ref[i, :, a, :]
-            edge = jnp.concatenate([edge, edge], axis=0).astype(jnp.bfloat16)
+            edge = volt_ref[i, :, a, :].astype(jnp.bfloat16)
             spread_ref[members * HALF :, lanes] = edge * left_ref[HALF : HALF + 1, lanes]
         grid_ref[...] = lax.dot_general(
             spread_ref[...], right_ref[...], (((1,), (1,)), ((), ())),
@@ -162,30 +174,31 @@
         for m in range(members):
             grid_ref[m * HALF : m * HALF + 1, GRID:] += grid_ref[
                 members * HALF + m : members * HALF + m + 1, 0:GRID]
-        for f in range(frames):
+        for f in range(CHUNK):
             for c in range(2):
                 m = 2 * f + c
                 for h in range(2):
-                    side_ref[f * GRID + h * HALF : f * GRID + (h + 1) * HALF, c * GRID : (c + 1) * GRID] = grid_ref[
+                    side_ref[i * CHUNK + f, h * HALF : (h + 1) * HALF, c * GRID : (c + 1) * GRID] = grid_ref[
                         m * HALF : (m + 1) * HALF, h * GRID : (h + 1) * GRID].astype(jnp.bfloat16)
-        half = jnp.dot(side_ref[...], first_ref[...], preferred_element_type=jnp.float32).astype(jnp.bfloat16)
-        for f in range(frames):
-            for c in range(2):
-                mid_ref[c * GRID : (c + 1) * GRID, f * GRID : (f + 1) * GRID] = half[
-                    f * GRID : (f + 1) * GRID, c * GRID : (c + 1) * GRID]
-        sky = jnp.dot(second_ref[...], mid_ref[...], preferred_element_type=jnp.float32)
-        power = sky[0:GRID] * sky[0:GRID] + sky[GRID:] * sky[GRID:]
-        total = power[:, 0:GRID]
-        for f in range(1, frames):
-            total = total + power[:, f * GRID : (f + 1) * GRID]
-        out_ref[i // blocks] += total * scale
         return carry
 
-    lax.fori_loop(0, 2 * blocks, chunk, 0)
-
-
-def whole(shape):
-    return pl.BlockSpec(shape, lambda: (0,) * len(shape))
+    lax.fori_loop(0, 2 * blocks * frames // CHUNK, chunk, 0)
+    for kk in range(2):
+        total = None
+        for t in range(blocks):
+            first = (kk * blocks + t) * frames
+            side = side_ref[first : first + frames].reshape(frames * GRID, 2 * GRID)
+            half = jnp.dot(side, first_ref[...], preferred_element_type=jnp.float32).astype(jnp.bfloat16)
+            mid = jnp.concatenate([
+                jnp.concatenate([
+                    half[f * GRID : (f + 1) * GRID, c * GRID : (c + 1) * GRID] for f in range(frames)], axis=1)
+                for c in range(2)], axis=0)
+            sky = jnp.dot(second_ref[...], mid, preferred_element_type=jnp.float32)
+            power = sky[0:GRID] * sky[0:GRID] + sky[GRID:] * sky[GRID:]
+            for f in range(frames):
+                part = power[:, f * GRID : (f + 1) * GRID]
+                total = part if total is None else total + part
+        out_ref[kk] = total * scale
 
 
 def local(voltages, calibrated_gain, cells, offsets):
@@ -199,12 +212,19 @@
     send = pl.pallas_call(
         lambda *refs: channelize_kernel(frames, *refs),
         out_shape=jax.ShapeDtypeStruct((rows, second), jnp.bfloat16),
+        in_specs=[pl.BlockSpec(memory_space=pl.ANY)] * 5,
         scratch_shapes=[
-            pltpu.VMEM((FIRST, (frames + TAPS - 1) * antennas, 2 * second), jnp.bfloat16),
+            pltpu.VMEM(voltages.shape, jnp.bfloat16),
+            pltpu.VMEM(calibrated_gain.shape, jnp.float32),
+            pltpu.VMEM((TAPS, channels), jnp.float32),
+            pltpu.VMEM((2, FIRST, second), jnp.float32),
+            pltpu.VMEM((2 * second, 2 * second), jnp.bfloat16),
+            pltpu.VMEM((FIRST * (frames + TAPS - 1) * antennas, 2 * second), jnp.bfloat16),
             pltpu.VMEM((channels, 128), jnp.float32),
             pltpu.VMEM((rows, second), jnp.float32),
+            pltpu.SemaphoreType.DMA((5,)),
         ],
-        compiler_params=pltpu.CompilerParams(vmem_limit_bytes=VMEM_BYTES),
+        compiler_params=pltpu.CompilerParams(vmem_limit_bytes=60 * 1024 * 1024),
         name="channelize",
     )(
         voltages, calibrated_gain, jnp.asarray(prototype(channels)),
@@ -229,17 +249,17 @@
     received = lax.all_to_all(send, ("chan", "tblk"), split_axis=0, concat_axis=0, tiled=True)
     received = received.reshape(rows, second)
 
-    members = 2 * frames
+    members = 2 * CHUNK
+    chunks = 2 * frames * lax.axis_size("tblk") // CHUNK
     return pl.pallas_call(
         lambda *refs: image_kernel(scale, *refs),
         out_shape=jax.ShapeDtypeStruct((2, GRID, GRID), jnp.float32),
         scratch_shapes=[
             pltpu.VMEM((rows, second), jnp.float32),
-            pltpu.VMEM((8, members, antennas, 128), jnp.float32),
+            pltpu.VMEM((chunks, members, antennas, 128), jnp.float32),
             pltpu.VMEM((members * HALF + 16, all_antennas), jnp.bfloat16),
             pltpu.VMEM((members * HALF + 16, 2 * GRID), jnp.float32),
-            pltpu.VMEM((frames * GRID, 2 * GRID), jnp.bfloat16),
-            pltpu.VMEM((2 * GRID, frames * GRID), jnp.bfloat16),
+            pltpu.VMEM((chunks * CHUNK, GRID, 2 * GRID), jnp.bfloat16),
         ],
         compiler_params=pltpu.CompilerParams(vmem_limit_bytes=VMEM_BYTES),
         name="image",

time: 63 us -> 55.8 us (0.89)
  local copies, waits for them, and re-layouts: 5.19 us -> 1.02 us
  Pallas kernels: 15.1 us -> 12.2 us
    unnamed x18 -> x8, local copies, waits for them, and re-layouts: 4.84 us -> 0.67 us
    pallas_call x1, Pallas kernels: 12.4 us -> 8.38 us  [local(): pl.pallas_call(lambda *refs: image_kernel(scale, *refs), out_shape=jax.Sh...]
    pallas_call x1, Pallas kernels: 2.11 us -> 3.24 us  [local(): pl.pallas_call(lambda *refs: channelize_kernel(frames, *refs), out_shape=...]
where the time goes in v2:
time: 55.8 us; the launch traced here: 55.5 us
  starting transfers between devices  22.2 us (40%)
  waiting for transfers between devices  20 us (36%)
  Pallas kernels  12.2 us (22%)
  local copies, waits for them, and re-layouts  1.02 us (2%)
    all_to_all x1, starting transfers between devices, local(): lax.all_to_all(send, ('chan', 'tblk'), split_axis=0, concat_axis=0, tiled...  22.2 us
    all_to_all x1, waiting for transfers between devices, local(): lax.all_to_all(send, ('chan', 'tblk'), split_axis=0, concat_axis=0, tiled...  20 us
    pallas_call x1, Pallas kernels, local(): pl.pallas_call(lambda *refs: image_kernel(scale, *refs), out_shape=jax.Sh...  8.38 us
    pallas_call x1, Pallas kernels, local(): pl.pallas_call(lambda *refs: channelize_kernel(frames, *refs), out_shape=...  3.24 us
  transfers between devices with their start and end apart: 1, of which 1 were waited for; matrix products, arithmetic and copies ran while one was open for 1% of the time, Pallas kernels for 1%

profile of v2, /device:TPU:1, one launch (start us, length us, event | category | flops | bytes accessed | tf_op | source)
XLA Modules:
  0.0 55.5 jit_solution(7056653643028468934)
XLA Ops:
  0.0 3.2 %channelize.1 = bf16[2048,128]{1,0:T(8,128)(2,1)} custom-call(bf16[2,4,16,1024]{3,2,1,0:T(8,128)(2,1)} %refs_0_.1, f32[2,16,1024]{2,1,0:T(8,128)} %refs_1_.1, f32[4,1024]{1,0:T(4,128)} %constant.8.clone.refs_2_, f32[2,8,128]{2,1,0:T(8,128)} %constant.9.clone.refs_3_, bf16[256,256]{1,0:T(8,128)(2,1)} %constant.10.clone.refs_4_.refs_3_), custom_call_target="tpu_custom_call" | custom-call | tf_op jit(solution)/shard_map/channelize/pallas_call | solution.py:212
  3.2 0.0 copy-start.2
  3.3 22.2 %all-to-all-start = ((bf16[512,4,128]{2,1,0:T(4,128)(2,1)}), bf16[512,4,128]{2,1,0:T(4,128)(2,1)S(1)}, u32[]{:S(2)}, u32[]{:S(2)}) async-start(bf16[512,4,128]{2,1,0:T(4,128)(2,1)} %bitcast.11), calls=%async_computation | async-start | bytes 1048576 | tf_op jit(solution)/shard_map/all_to_all | solution.py:249
  25.4 0.0 copy-done.2
  25.4 0.1 reshape.20
  25.6 0.0 copy-start.3
  25.6 0.1 copy.12
  25.6 0.6 %copy-done.3 = s32[2,2048]{1,0:T(2,128)S(1)} copy-done((s32[2,2048]{1,0:T(2,128)S(1)}, s32[2,2048]{1,0:T(2,128)}, u32[]{:S(2)}) %copy-start.3) | copy-done | bytes 16408
  26.3 0.1 reshape.22
  26.4 0.0 copy-start
  26.4 0.0 copy-start.1
  26.4 0.1 copy.13
  26.5 0.6 %footprint.1 = (bf16[256,2048]{1,0:T(8,128)(2,1)S(1)}, bf16[80,2048]{1,0:T(8,128)(2,1)S(1)}) custom-call(s32[2,2048]{1,0:T(2,128)S(1)} %get-tuple-element.10.cells_ref, s32[2,2048]{1,0:T(2,128)S(1)} %get-tuple-element.9.offsets_ref), custom_call_target="tpu_custom_call" | custom-call | flops 10000000 | bytes 1500000 | tf_op jit(solution)/shard_map/footprint/pallas_call | solution.py:237
  27.1 20.0 %all-to-all-done = bf16[512,4,128]{2,1,0:T(4,128)(2,1)S(1)} async-done(((bf16[512,4,128]{2,1,0:T(4,128)(2,1)}), bf16[512,4,128]{2,1,0:T(4,128)(2,1)S(1)}, u32[]{:S(2)}, u32[]{:S(2)}) %all-to-all-start) | async-done | bytes 524320 | tf_op jit(solution)/shard_map/all_to_all | solution.py:249
  47.1 0.0 copy-done
  47.1 0.0 copy-done.1
  47.2 8.4 %image.1 = f32[2,128,128]{2,1,0:T(8,128)} custom-call(bf16[2048,128]{1,0:T(8,128)(2,1)S(1)} %bitcast.10, bf16[256,2048]{1,0:T(8,128)(2,1)S(1)} %get-tuple-element.7.refs_1_, bf16[80,2048]{1,0:T(8,128)(2,1)S(1)} %get-tuple-element.8.refs_2_, bf16[256,256]{1,0:T(8,128)(2,1)S(1)} %copy-done, bf16[256,256]{1,0:T(8,128)(2,1)S(1)} %copy-done.1), custom_call_target="tpu_custom_call" | custom-call | tf_op jit(solution)/shard_map/image/pallas_call | solution.py:254
  (1 shorter events, 0.0 us)
Async XLA Ops:
  3.2 22.2 %copy-start.2 = (s32[2,2048]{1,0:T(2,128)S(1)}, s32[2,2048]{1,0:T(2,128)}, u32[]{:S(2)}) copy-start(s32[2,2048]{1,0:T(2,128)} %param.11) | copy-start | bytes 49156
  3.3 43.9 %all-to-all-start = ((bf16[512,4,128]{2,1,0:T(4,128)(2,1)}), bf16[512,4,128]{2,1,0:T(4,128)(2,1)S(1)}, u32[]{:S(2)}, u32[]{:S(2)}) async-start(bf16[512,4,128]{2,1,0:T(4,128)(2,1)} %bitcast.11), calls=%async_computation | async-start | bytes 1048576 | tf_op jit(solution)/shard_map/all_to_all | solution.py:249
  25.6 0.7 %copy-start.3 = (s32[2,2048]{1,0:T(2,128)S(1)}, s32[2,2048]{1,0:T(2,128)}, u32[]{:S(2)}) copy-start(s32[2,2048]{1,0:T(2,128)} %param.12) | copy-start | bytes 49156
  26.4 20.8 %copy-start = (bf16[256,256]{1,0:T(8,128)(2,1)S(1)}, bf16[256,256]{1,0:T(8,128)(2,1)}, u32[]{:S(2)}) copy-start(bf16[256,256]{1,0:T(8,128)(2,1)} %constant.10.clone.refs_4_.refs_3_) | copy-start | bytes 393220
  26.4 20.8 %copy-start.1 = (bf16[256,256]{1,0:T(8,128)(2,1)S(1)}, bf16[256,256]{1,0:T(8,128)(2,1)}, u32[]{:S(2)}) copy-start(bf16[256,256]{1,0:T(8,128)(2,1)} %constant.11.clone.refs_4_) | copy-start | bytes 393220

commit v3 on v2

--- a/solution.py
+++ b/solution.py
@@ -11,8 +11,9 @@
 GRID = 128
 TAPS = 4
 FIRST = 8
-HALF = GRID // 2
-CHUNK = 8
+BANDS = 4
+BAND = GRID // BANDS
+CHUNK = 16
 VMEM_BYTES = 32 * 1024 * 1024
 
 
@@ -123,16 +124,15 @@
     rows, cols = cells_ref[0:1, :], cells_ref[1:2, :]
     share = (offsets_ref[...].astype(jnp.float32) + 0.5) * 0.125
     t_row, t_col = share[0:1, :], share[1:2, :]
-    upper = (rows >= HALF).astype(jnp.int32)
-    low = rows - upper * HALF
-    place = upper * GRID + cols
+    low = rows & (BAND - 1)
+    place = (rows - low) * (GRID // BAND) + cols
 
     def table(height, first, weight):
         at = lax.broadcasted_iota(jnp.int32, (height, count), 0)
         near = jnp.where(at == first, 1.0 - weight, 0.0)
         return jnp.where(at == first + 1, weight, near).astype(jnp.bfloat16)
 
-    right_ref[...] = table(2 * GRID, place, t_col)
+    right_ref[...] = table(BANDS * GRID, place, t_col)
     left_ref[...] = table(left_ref.shape[0], low, t_row)
 
 
@@ -162,24 +162,24 @@
     def chunk(i, carry):
         for a in range(antennas):
             lanes = slice(a * 128, (a + 1) * 128)
-            left = left_ref[0:HALF, lanes]
+            left = left_ref[0:BAND, lanes]
             for m in range(members):
                 row = volt_ref[i, m, a : a + 1, :].astype(jnp.bfloat16)
-                spread_ref[m * HALF : (m + 1) * HALF, lanes] = left * row
+                spread_ref[m * BAND : (m + 1) * BAND, lanes] = left * row
             edge = volt_ref[i, :, a, :].astype(jnp.bfloat16)
-            spread_ref[members * HALF :, lanes] = edge * left_ref[HALF : HALF + 1, lanes]
+            spread_ref[members * BAND :, lanes] = edge * left_ref[BAND : BAND + 1, lanes]
         grid_ref[...] = lax.dot_general(
             spread_ref[...], right_ref[...], (((1,), (1,)), ((), ())),
             preferred_element_type=jnp.float32)
         for m in range(members):
-            grid_ref[m * HALF : m * HALF + 1, GRID:] += grid_ref[
-                members * HALF + m : members * HALF + m + 1, 0:GRID]
+            grid_ref[m * BAND : m * BAND + 1, GRID:] += grid_ref[
+                members * BAND + m : members * BAND + m + 1, : (BANDS - 1) * GRID]
         for f in range(CHUNK):
             for c in range(2):
                 m = 2 * f + c
-                for h in range(2):
-                    side_ref[i * CHUNK + f, h * HALF : (h + 1) * HALF, c * GRID : (c + 1) * GRID] = grid_ref[
-                        m * HALF : (m + 1) * HALF, h * GRID : (h + 1) * GRID].astype(jnp.bfloat16)
+                for h in range(BANDS):
+                    side_ref[i * CHUNK + f, h * BAND : (h + 1) * BAND, c * GRID : (c + 1) * GRID] = grid_ref[
+                        m * BAND : (m + 1) * BAND, h * GRID : (h + 1) * GRID].astype(jnp.bfloat16)
         return carry
 
     lax.fori_loop(0, 2 * blocks * frames // CHUNK, chunk, 0)
@@ -237,8 +237,8 @@
     right, left = pl.pallas_call(
         footprint_kernel,
         out_shape=(
-            jax.ShapeDtypeStruct((2 * GRID, all_antennas), jnp.bfloat16),
-            jax.ShapeDtypeStruct((HALF + 16, all_antennas), jnp.bfloat16),
+            jax.ShapeDtypeStruct((BANDS * GRID, all_antennas), jnp.bfloat16),
+            jax.ShapeDtypeStruct((BAND + 16, all_antennas), jnp.bfloat16),
         ),
         compiler_params=pltpu.CompilerParams(vmem_limit_bytes=VMEM_BYTES),
         cost_estimate=pl.CostEstimate(flops=10_000_000, bytes_accessed=1_500_000, transcendentals=0),
@@ -257,8 +257,8 @@
         scratch_shapes=[
             pltpu.VMEM((rows, second), jnp.float32),
             pltpu.VMEM((chunks, members, antennas, 128), jnp.float32),
-            pltpu.VMEM((members * HALF + 16, all_antennas), jnp.bfloat16),
-            pltpu.VMEM((members * HALF + 16, 2 * GRID), jnp.float32),
+            pltpu.VMEM((members * (BAND + 1), all_antennas), jnp.bfloat16),
+            pltpu.VMEM((members * (BAND + 1), BANDS * GRID), jnp.float32),
             pltpu.VMEM((chunks * CHUNK, GRID, 2 * GRID), jnp.bfloat16),
         ],
         compiler_params=pltpu.CompilerParams(vmem_limit_bytes=VMEM_BYTES),

time: 55.8 us -> 55 us (0.986)
  local copies, waits for them, and re-layouts: 1.02 us -> 0.38 us
    pallas_call x1, Pallas kernels: 8.38 us -> 7.61 us  [local(): pl.pallas_call(lambda *refs: image_kernel(scale, *refs), out_shape=jax.Sh...]
    unnamed x8, local copies, waits for them, and re-layouts: 0.67 us -> 0.02 us
  transfers between devices with their start and end apart: 1 -> 1, of which waited for: 1 -> 1; matrix products, arithmetic and copies ran while one was open for 1% -> 1% of each run, Pallas kernels for 1% -> 2%
where the time goes in v3:
time: 55 us; the launch traced here: 54.8 us
  starting transfers between devices  22.2 us (40%)
  waiting for transfers between devices  20.3 us (37%)
  Pallas kernels  11.9 us (22%)
    all_to_all x1, starting transfers between devices, local(): lax.all_to_all(send, ('chan', 'tblk'), split_axis=0, concat_axis=0, tiled...  22.2 us
    all_to_all x1, waiting for transfers between devices, local(): lax.all_to_all(send, ('chan', 'tblk'), split_axis=0, concat_axis=0, tiled...  20.3 us
    pallas_call x1, Pallas kernels, local(): pl.pallas_call(lambda *refs: image_kernel(scale, *refs), out_shape=jax.Sh...  7.61 us
    pallas_call x1, Pallas kernels, local(): pl.pallas_call(lambda *refs: channelize_kernel(frames, *refs), out_shape=...  3.29 us
  transfers between devices with their start and end apart: 1, of which 1 were waited for; matrix products, arithmetic and copies ran while one was open for 1% of the time, Pallas kernels for 2%

profile of v3, /device:TPU:1, one launch (start us, length us, event | category | flops | bytes accessed | tf_op | source)
XLA Modules:
  0.0 54.8 jit_solution(6259318576278844789)
XLA Ops:
  0.0 0.0 copy-start
  0.0 0.0 copy-start.1
  0.0 0.0 copy-start.2
  0.0 0.0 copy-start.3
  0.0 3.3 %channelize.1 = bf16[2048,128]{1,0:T(8,128)(2,1)} custom-call(bf16[2,4,16,1024]{3,2,1,0:T(8,128)(2,1)} %refs_0_.1, f32[2,16,1024]{2,1,0:T(8,128)} %refs_1_.1, f32[4,1024]{1,0:T(4,128)} %constant.8.clone.refs_2_, f32[2,8,128]{2,1,0:T(8,128)} %constant.9.clone.refs_3_, bf16[256,256]{1,0:T(8,128)(2,1)} %constant.10.clone.refs_4_.refs_3_), custom_call_target="tpu_custom_call" | custom-call | tf_op jit(solution)/shard_map/channelize/pallas_call | solution.py:212
  3.3 22.2 %all-to-all-start = ((bf16[512,4,128]{2,1,0:T(4,128)(2,1)}), bf16[512,4,128]{2,1,0:T(4,128)(2,1)S(1)}, u32[]{:S(2)}, u32[]{:S(2)}) async-start(bf16[512,4,128]{2,1,0:T(4,128)(2,1)} %bitcast.11), calls=%async_computation | async-start | bytes 1048576 | tf_op jit(solution)/shard_map/all_to_all | solution.py:249
  25.5 0.0 copy-done.2
  25.5 0.1 reshape.20
  25.6 0.1 copy.12
  25.7 0.0 copy-done.3
  25.7 0.1 reshape.22
  25.8 0.1 copy.13
  25.9 1.0 %footprint.1 = (bf16[512,2048]{1,0:T(8,128)(2,1)S(1)}, bf16[48,2048]{1,0:T(8,128)(2,1)S(1)}) custom-call(s32[2,2048]{1,0:T(2,128)S(1)} %get-tuple-element.10.cells_ref, s32[2,2048]{1,0:T(2,128)S(1)} %get-tuple-element.9.offsets_ref), custom_call_target="tpu_custom_call" | custom-call | flops 10000000 | bytes 1500000 | tf_op jit(solution)/shard_map/footprint/pallas_call | solution.py:237
  26.9 20.3 %all-to-all-done = bf16[512,4,128]{2,1,0:T(4,128)(2,1)S(1)} async-done(((bf16[512,4,128]{2,1,0:T(4,128)(2,1)}), bf16[512,4,128]{2,1,0:T(4,128)(2,1)S(1)}, u32[]{:S(2)}, u32[]{:S(2)}) %all-to-all-start) | async-done | bytes 524320 | tf_op jit(solution)/shard_map/all_to_all | solution.py:249
  47.2 0.0 copy-done
  47.2 0.0 copy-done.1
  47.2 7.6 %image.1 = f32[2,128,128]{2,1,0:T(8,128)} custom-call(bf16[2048,128]{1,0:T(8,128)(2,1)S(1)} %bitcast.10, bf16[512,2048]{1,0:T(8,128)(2,1)S(1)} %get-tuple-element.7.refs_1_, bf16[48,2048]{1,0:T(8,128)(2,1)S(1)} %get-tuple-element.8.refs_2_, bf16[256,256]{1,0:T(8,128)(2,1)S(1)} %copy-done, bf16[256,256]{1,0:T(8,128)(2,1)S(1)} %copy-done.1), custom_call_target="tpu_custom_call" | custom-call | tf_op jit(solution)/shard_map/image/pallas_call | solution.py:254
  (1 shorter events, 0.0 us)
Async XLA Ops:
  0.0 47.2 %copy-start = (bf16[256,256]{1,0:T(8,128)(2,1)S(1)}, bf16[256,256]{1,0:T(8,128)(2,1)}, u32[]{:S(2)}) copy-start(bf16[256,256]{1,0:T(8,128)(2,1)} %constant.10.clone.refs_4_.refs_3_) | copy-start | bytes 393220
  0.0 47.2 %copy-start.1 = (bf16[256,256]{1,0:T(8,128)(2,1)S(1)}, bf16[256,256]{1,0:T(8,128)(2,1)}, u32[]{:S(2)}) copy-start(bf16[256,256]{1,0:T(8,128)(2,1)} %constant.11.clone.refs_4_) | copy-start | bytes 393220
  0.0 25.5 %copy-start.2 = (s32[2,2048]{1,0:T(2,128)S(1)}, s32[2,2048]{1,0:T(2,128)}, u32[]{:S(2)}) copy-start(s32[2,2048]{1,0:T(2,128)} %param.11) | copy-start | bytes 49156
  0.0 25.7 %copy-start.3 = (s32[2,2048]{1,0:T(2,128)S(1)}, s32[2,2048]{1,0:T(2,128)}, u32[]{:S(2)}) copy-start(s32[2,2048]{1,0:T(2,128)} %param.12) | copy-start | bytes 49156
  3.3 43.9 %all-to-all-start = ((bf16[512,4,128]{2,1,0:T(4,128)(2,1)}), bf16[512,4,128]{2,1,0:T(4,128)(2,1)S(1)}, u32[]{:S(2)}, u32[]{:S(2)}) async-start(bf16[512,4,128]{2,1,0:T(4,128)(2,1)} %bitcast.11), calls=%async_computation | async-start | bytes 1048576 | tf_op jit(solution)/shard_map/all_to_all | solution.py:249

commit v4 on v3

--- a/solution.py
+++ b/solution.py
@@ -13,6 +13,7 @@
 FIRST = 8
 BANDS = 4
 BAND = GRID // BANDS
+GROUP = 8
 CHUNK = 16
 VMEM_BYTES = 32 * 1024 * 1024
 
@@ -103,7 +104,7 @@
             part_ref[row : row + antennas, second:] = out_im.astype(jnp.bfloat16)
     copies[3].wait()
     both = jnp.concatenate([gain_ref[0], gain_ref[1]], axis=0)
-    turn_ref[:, 0 : 2 * antennas] = both.T
+    turn_ref[0:channels, 0 : 2 * antennas] = both.T
     copies[4].wait()
     blank = jnp.zeros(((2 * frames - spans) * antennas, second), jnp.float32)
     all_spectra = jnp.dot(part_ref[...], table_ref[...], preferred_element_type=jnp.float32)
@@ -116,7 +117,7 @@
         for c, volts in enumerate((re * gain_re - im * gain_im, re * gain_im + im * gain_re)):
             turned = jnp.concatenate([volts, blank], axis=0).T
             sorted_ref[pl.ds(2 * k + c, second, stride=2 * FIRST), :] = turned
-    out_ref[...] = sorted_ref[...].astype(jnp.bfloat16)
+    out_ref[...] = sorted_ref[0 : out_ref.shape[0]].astype(jnp.bfloat16)
 
 
 def footprint_kernel(cells_ref, offsets_ref, right_ref, left_ref):
@@ -142,7 +143,7 @@
     frames = 4
     antennas = 16
     step = 4 * blocks
-    wide_ref[...] = x_ref[...].astype(jnp.float32)
+    wide_ref[0 : x_ref.shape[0]] = x_ref[...].astype(jnp.float32)
     for kk in range(2):
         for c in range(2):
             tail = None
@@ -185,17 +186,17 @@
     lax.fori_loop(0, 2 * blocks * frames // CHUNK, chunk, 0)
     for kk in range(2):
         total = None
-        for t in range(blocks):
-            first = (kk * blocks + t) * frames
-            side = side_ref[first : first + frames].reshape(frames * GRID, 2 * GRID)
+        for t in range(0, blocks * frames, GROUP):
+            first = kk * blocks * frames + t
+            side = side_ref[first : first + GROUP].reshape(GROUP * GRID, 2 * GRID)
             half = jnp.dot(side, first_ref[...], preferred_element_type=jnp.float32).astype(jnp.bfloat16)
             mid = jnp.concatenate([
                 jnp.concatenate([
-                    half[f * GRID : (f + 1) * GRID, c * GRID : (c + 1) * GRID] for f in range(frames)], axis=1)
+                    half[f * GRID : (f + 1) * GRID, c * GRID : (c + 1) * GRID] for f in range(GROUP)], axis=1)
                 for c in range(2)], axis=0)
             sky = jnp.dot(second_ref[...], mid, preferred_element_type=jnp.float32)
             power = sky[0:GRID] * sky[0:GRID] + sky[GRID:] * sky[GRID:]
-            for f in range(frames):
+            for f in range(GROUP):
                 part = power[:, f * GRID : (f + 1) * GRID]
                 total = part if total is None else total + part
         out_ref[kk] = total * scale
@@ -220,8 +221,8 @@
             pltpu.VMEM((2, FIRST, second), jnp.float32),
             pltpu.VMEM((2 * second, 2 * second), jnp.bfloat16),
             pltpu.VMEM((FIRST * (frames + TAPS - 1) * antennas, 2 * second), jnp.bfloat16),
-            pltpu.VMEM((channels, 128), jnp.float32),
-            pltpu.VMEM((rows, second), jnp.float32),
+            pltpu.VMEM((channels + FIRST, 128), jnp.float32),
+            pltpu.VMEM((rows + 2 * FIRST, second), jnp.float32),
             pltpu.SemaphoreType.DMA((5,)),
         ],
         compiler_params=pltpu.CompilerParams(vmem_limit_bytes=60 * 1024 * 1024),
@@ -255,7 +256,7 @@
         lambda *refs: image_kernel(scale, *refs),
         out_shape=jax.ShapeDtypeStruct((2, GRID, GRID), jnp.float32),
         scratch_shapes=[
-            pltpu.VMEM((rows, second), jnp.float32),
+            pltpu.VMEM((rows + 16, second), jnp.float32),
             pltpu.VMEM((chunks, members, antennas, 128), jnp.float32),
             pltpu.VMEM((members * (BAND + 1), all_antennas), jnp.bfloat16),
             pltpu.VMEM((members * (BAND + 1), BANDS * GRID), jnp.float32),

time: 55 us -> 55 us (level)
  no operation moved by 1% of the time
where the time goes in v4:
time: 55 us; the launch traced here: 54.9 us
  starting transfers between devices  22.2 us (40%)
  waiting for transfers between devices  20.3 us (37%)
  Pallas kernels  11.9 us (22%)
    all_to_all x1, starting transfers between devices, local(): lax.all_to_all(send, ('chan', 'tblk'), split_axis=0, concat_axis=0, tiled...  22.2 us
    all_to_all x1, waiting for transfers between devices, local(): lax.all_to_all(send, ('chan', 'tblk'), split_axis=0, concat_axis=0, tiled...  20.3 us
    pallas_call x1, Pallas kernels, local(): pl.pallas_call(lambda *refs: image_kernel(scale, *refs), out_shape=jax.Sh...  7.65 us
    pallas_call x1, Pallas kernels, local(): pl.pallas_call(lambda *refs: channelize_kernel(frames, *refs), out_shape=...  3.29 us
  transfers between devices with their start and end apart: 1, of which 1 were waited for; matrix products, arithmetic and copies ran while one was open for 1% of the time, Pallas kernels for 2%

profile of v4, /device:TPU:1, one launch (start us, length us, event | category | flops | bytes accessed | tf_op | source)
XLA Modules:
  0.0 54.9 jit_solution(5414959484312184720)
XLA Ops:
  0.0 0.0 copy-start
  0.0 0.0 copy-start.1
  0.0 0.0 copy-start.2
  0.0 0.0 copy-start.3
  0.0 3.3 %channelize.1 = bf16[2048,128]{1,0:T(8,128)(2,1)} custom-call(bf16[2,4,16,1024]{3,2,1,0:T(8,128)(2,1)} %refs_0_.1, f32[2,16,1024]{2,1,0:T(8,128)} %refs_1_.1, f32[4,1024]{1,0:T(4,128)} %constant.8.clone.refs_2_, f32[2,8,128]{2,1,0:T(8,128)} %constant.9.clone.refs_3_, bf16[256,256]{1,0:T(8,128)(2,1)} %constant.10.clone.refs_4_.refs_3_), custom_call_target="tpu_custom_call" | custom-call | tf_op jit(solution)/shard_map/channelize/pallas_call | solution.py:213
  3.3 22.2 %all-to-all-start = ((bf16[512,4,128]{2,1,0:T(4,128)(2,1)}), bf16[512,4,128]{2,1,0:T(4,128)(2,1)S(1)}, u32[]{:S(2)}, u32[]{:S(2)}) async-start(bf16[512,4,128]{2,1,0:T(4,128)(2,1)} %bitcast.11), calls=%async_computation | async-start | bytes 1048576 | tf_op jit(solution)/shard_map/all_to_all | solution.py:250
  25.5 0.0 copy-done.2
  25.5 0.1 reshape.20
  25.6 0.1 copy.12
  25.7 0.0 copy-done.3
  25.7 0.1 reshape.22
  25.8 0.1 copy.13
  25.9 1.0 %footprint.1 = (bf16[512,2048]{1,0:T(8,128)(2,1)S(1)}, bf16[48,2048]{1,0:T(8,128)(2,1)S(1)}) custom-call(s32[2,2048]{1,0:T(2,128)S(1)} %get-tuple-element.10.cells_ref, s32[2,2048]{1,0:T(2,128)S(1)} %get-tuple-element.9.offsets_ref), custom_call_target="tpu_custom_call" | custom-call | flops 10000000 | bytes 1500000 | tf_op jit(solution)/shard_map/footprint/pallas_call | solution.py:238
  26.9 20.3 %all-to-all-done = bf16[512,4,128]{2,1,0:T(4,128)(2,1)S(1)} async-done(((bf16[512,4,128]{2,1,0:T(4,128)(2,1)}), bf16[512,4,128]{2,1,0:T(4,128)(2,1)S(1)}, u32[]{:S(2)}, u32[]{:S(2)}) %all-to-all-start) | async-done | bytes 524320 | tf_op jit(solution)/shard_map/all_to_all | solution.py:250
  47.2 0.0 copy-done
  47.2 0.0 copy-done.1
  47.2 7.7 %image.1 = f32[2,128,128]{2,1,0:T(8,128)} custom-call(bf16[2048,128]{1,0:T(8,128)(2,1)S(1)} %bitcast.10, bf16[512,2048]{1,0:T(8,128)(2,1)S(1)} %get-tuple-element.7.refs_1_, bf16[48,2048]{1,0:T(8,128)(2,1)S(1)} %get-tuple-element.8.refs_2_, bf16[256,256]{1,0:T(8,128)(2,1)S(1)} %copy-done, bf16[256,256]{1,0:T(8,128)(2,1)S(1)} %copy-done.1), custom_call_target="tpu_custom_call" | custom-call | tf_op jit(solution)/shard_map/image/pallas_call | solution.py:255
  (1 shorter events, 0.0 us)
Async XLA Ops:
  0.0 47.2 %copy-start = (bf16[256,256]{1,0:T(8,128)(2,1)S(1)}, bf16[256,256]{1,0:T(8,128)(2,1)}, u32[]{:S(2)}) copy-start(bf16[256,256]{1,0:T(8,128)(2,1)} %constant.10.clone.refs_4_.refs_3_) | copy-start | bytes 393220
  0.0 47.2 %copy-start.1 = (bf16[256,256]{1,0:T(8,128)(2,1)S(1)}, bf16[256,256]{1,0:T(8,128)(2,1)}, u32[]{:S(2)}) copy-start(bf16[256,256]{1,0:T(8,128)(2,1)} %constant.11.clone.refs_4_) | copy-start | bytes 393220
  0.0 25.5 %copy-start.2 = (s32[2,2048]{1,0:T(2,128)S(1)}, s32[2,2048]{1,0:T(2,128)}, u32[]{:S(2)}) copy-start(s32[2,2048]{1,0:T(2,128)} %param.11) | copy-start | bytes 49156
  0.0 25.7 %copy-start.3 = (s32[2,2048]{1,0:T(2,128)S(1)}, s32[2,2048]{1,0:T(2,128)}, u32[]{:S(2)}) copy-start(s32[2,2048]{1,0:T(2,128)} %param.12) | copy-start | bytes 49156
  3.3 43.9 %all-to-all-start = ((bf16[512,4,128]{2,1,0:T(4,128)(2,1)}), bf16[512,4,128]{2,1,0:T(4,128)(2,1)S(1)}, u32[]{:S(2)}, u32[]{:S(2)}) async-start(bf16[512,4,128]{2,1,0:T(4,128)(2,1)} %bitcast.11), calls=%async_computation | async-start | bytes 1048576 | tf_op jit(solution)/shard_map/all_to_all | solution.py:250

commit v5 on v4

--- a/solution.py
+++ b/solution.py
@@ -13,6 +13,8 @@
 FIRST = 8
 BANDS = 4
 BAND = GRID // BANDS
+OUT_PITCH = 24
+IN_PITCH = 17
 GROUP = 8
 CHUNK = 16
 VMEM_BYTES = 32 * 1024 * 1024
@@ -116,8 +118,11 @@
         re, im = spectra[:, 0:second], spectra[:, second:]
         for c, volts in enumerate((re * gain_re - im * gain_im, re * gain_im + im * gain_re)):
             turned = jnp.concatenate([volts, blank], axis=0).T
-            sorted_ref[pl.ds(2 * k + c, second, stride=2 * FIRST), :] = turned
-    out_ref[...] = sorted_ref[0 : out_ref.shape[0]].astype(jnp.bfloat16)
+            sorted_ref[pl.ds(2 * k + c, second, stride=OUT_PITCH), :] = turned
+    width = 2 * FIRST
+    for d in range(second):
+        out_ref[d * width : (d + 1) * width] = sorted_ref[
+            d * OUT_PITCH : d * OUT_PITCH + width].astype(jnp.bfloat16)
 
 
 def footprint_kernel(cells_ref, offsets_ref, right_ref, left_ref):
@@ -143,12 +148,13 @@
     frames = 4
     antennas = 16
     step = 4 * blocks
-    wide_ref[0 : x_ref.shape[0]] = x_ref[...].astype(jnp.float32)
+    for d in range(128):
+        wide_ref[d * IN_PITCH : d * IN_PITCH + step] = x_ref[d * step : (d + 1) * step].astype(jnp.float32)
     for kk in range(2):
         for c in range(2):
             tail = None
             for t in range(blocks):
-                turned = wide_ref[pl.ds(4 * t + 2 * kk + c, 128, stride=step), :].T
+                turned = wide_ref[pl.ds(4 * t + 2 * kk + c, 128, stride=IN_PITCH), :].T
                 own = turned[0 : frames * antennas]
                 if tail is not None:
                     own = jnp.concatenate(
@@ -222,7 +228,7 @@
             pltpu.VMEM((2 * second, 2 * second), jnp.bfloat16),
             pltpu.VMEM((FIRST * (frames + TAPS - 1) * antennas, 2 * second), jnp.bfloat16),
             pltpu.VMEM((channels + FIRST, 128), jnp.float32),
-            pltpu.VMEM((rows + 2 * FIRST, second), jnp.float32),
+            pltpu.VMEM((second * OUT_PITCH + 2 * FIRST, second), jnp.float32),
             pltpu.SemaphoreType.DMA((5,)),
         ],
         compiler_params=pltpu.CompilerParams(vmem_limit_bytes=60 * 1024 * 1024),
@@ -256,7 +262,7 @@
         lambda *refs: image_kernel(scale, *refs),
         out_shape=jax.ShapeDtypeStruct((2, GRID, GRID), jnp.float32),
         scratch_shapes=[
-            pltpu.VMEM((rows + 16, second), jnp.float32),
+            pltpu.VMEM((128 * IN_PITCH + 16, second), jnp.float32),
             pltpu.VMEM((chunks, members, antennas, 128), jnp.float32),
             pltpu.VMEM((members * (BAND + 1), all_antennas), jnp.bfloat16),
             pltpu.VMEM((members * (BAND + 1), BANDS * GRID), jnp.float32),

time: 55 us -> 54.7 us (level)
  no operation moved by 1% of the time
where the time goes in v5:
time: 54.7 us; the launch traced here: 54.6 us
  starting transfers between devices  22.2 us (41%)
  waiting for transfers between devices  20.3 us (37%)
  Pallas kernels  11.6 us (21%)
    all_to_all x1, starting transfers between devices, local(): lax.all_to_all(send, ('chan', 'tblk'), split_axis=0, concat_axis=0, tiled...  22.2 us
    all_to_all x1, waiting for transfers between devices, local(): lax.all_to_all(send, ('chan', 'tblk'), split_axis=0, concat_axis=0, tiled...  20.3 us
    pallas_call x1, Pallas kernels, local(): pl.pallas_call(lambda *refs: image_kernel(scale, *refs), out_shape=jax.Sh...  7.46 us
    pallas_call x1, Pallas kernels, local(): pl.pallas_call(lambda *refs: channelize_kernel(frames, *refs), out_shape=...  3.2 us
  transfers between devices with their start and end apart: 1, of which 1 were waited for; matrix products, arithmetic and copies ran while one was open for 1% of the time, Pallas kernels for 2%

profile of v5, /device:TPU:1, one launch (start us, length us, event | category | flops | bytes accessed | tf_op | source)
XLA Modules:
  0.0 54.6 jit_solution(7331876794259321608)
XLA Ops:
  0.0 0.0 copy-start
  0.0 0.0 copy-start.1
  0.0 0.0 copy-start.2
  0.0 0.0 copy-start.3
  0.0 3.2 %channelize.1 = bf16[2048,128]{1,0:T(8,128)(2,1)} custom-call(bf16[2,4,16,1024]{3,2,1,0:T(8,128)(2,1)} %refs_0_.1, f32[2,16,1024]{2,1,0:T(8,128)} %refs_1_.1, f32[4,1024]{1,0:T(4,128)} %constant.8.clone.refs_2_, f32[2,8,128]{2,1,0:T(8,128)} %constant.9.clone.refs_3_, bf16[256,256]{1,0:T(8,128)(2,1)} %constant.10.clone.refs_4_.refs_3_), custom_call_target="tpu_custom_call" | custom-call | tf_op jit(solution)/shard_map/channelize/pallas_call | solution.py:219
  3.2 22.2 %all-to-all-start = ((bf16[512,4,128]{2,1,0:T(4,128)(2,1)}), bf16[512,4,128]{2,1,0:T(4,128)(2,1)S(1)}, u32[]{:S(2)}, u32[]{:S(2)}) async-start(bf16[512,4,128]{2,1,0:T(4,128)(2,1)} %bitcast.11), calls=%async_computation | async-start | bytes 1048576 | tf_op jit(solution)/shard_map/all_to_all | solution.py:256
  25.4 0.0 copy-done.2
  25.4 0.1 reshape.20
  25.5 0.1 copy.12
  25.6 0.0 copy-done.3
  25.6 0.1 reshape.22
  25.7 0.1 copy.13
  25.8 1.0 %footprint.1 = (bf16[512,2048]{1,0:T(8,128)(2,1)S(1)}, bf16[48,2048]{1,0:T(8,128)(2,1)S(1)}) custom-call(s32[2,2048]{1,0:T(2,128)S(1)} %get-tuple-element.10.cells_ref, s32[2,2048]{1,0:T(2,128)S(1)} %get-tuple-element.9.offsets_ref), custom_call_target="tpu_custom_call" | custom-call | flops 10000000 | bytes 1500000 | tf_op jit(solution)/shard_map/footprint/pallas_call | solution.py:244
  26.8 20.3 %all-to-all-done = bf16[512,4,128]{2,1,0:T(4,128)(2,1)S(1)} async-done(((bf16[512,4,128]{2,1,0:T(4,128)(2,1)}), bf16[512,4,128]{2,1,0:T(4,128)(2,1)S(1)}, u32[]{:S(2)}, u32[]{:S(2)}) %all-to-all-start) | async-done | bytes 524320 | tf_op jit(solution)/shard_map/all_to_all | solution.py:256
  47.1 0.0 copy-done
  47.1 0.0 copy-done.1
  47.1 7.5 %image.1 = f32[2,128,128]{2,1,0:T(8,128)} custom-call(bf16[2048,128]{1,0:T(8,128)(2,1)S(1)} %bitcast.10, bf16[512,2048]{1,0:T(8,128)(2,1)S(1)} %get-tuple-element.7.refs_1_, bf16[48,2048]{1,0:T(8,128)(2,1)S(1)} %get-tuple-element.8.refs_2_, bf16[256,256]{1,0:T(8,128)(2,1)S(1)} %copy-done, bf16[256,256]{1,0:T(8,128)(2,1)S(1)} %copy-done.1), custom_call_target="tpu_custom_call" | custom-call | tf_op jit(solution)/shard_map/image/pallas_call | solution.py:261
  (1 shorter events, 0.0 us)
Async XLA Ops:
  0.0 47.1 %copy-start = (bf16[256,256]{1,0:T(8,128)(2,1)S(1)}, bf16[256,256]{1,0:T(8,128)(2,1)}, u32[]{:S(2)}) copy-start(bf16[256,256]{1,0:T(8,128)(2,1)} %constant.10.clone.refs_4_.refs_3_) | copy-start | bytes 393220
  0.0 47.1 %copy-start.1 = (bf16[256,256]{1,0:T(8,128)(2,1)S(1)}, bf16[256,256]{1,0:T(8,128)(2,1)}, u32[]{:S(2)}) copy-start(bf16[256,256]{1,0:T(8,128)(2,1)} %constant.11.clone.refs_4_) | copy-start | bytes 393220
  0.0 25.4 %copy-start.2 = (s32[2,2048]{1,0:T(2,128)S(1)}, s32[2,2048]{1,0:T(2,128)}, u32[]{:S(2)}) copy-start(s32[2,2048]{1,0:T(2,128)} %param.11) | copy-start | bytes 49156
  0.0 25.6 %copy-start.3 = (s32[2,2048]{1,0:T(2,128)S(1)}, s32[2,2048]{1,0:T(2,128)}, u32[]{:S(2)}) copy-start(s32[2,2048]{1,0:T(2,128)} %param.12) | copy-start | bytes 49156
  3.2 43.9 %all-to-all-start = ((bf16[512,4,128]{2,1,0:T(4,128)(2,1)}), bf16[512,4,128]{2,1,0:T(4,128)(2,1)S(1)}, u32[]{:S(2)}, u32[]{:S(2)}) async-start(bf16[512,4,128]{2,1,0:T(4,128)(2,1)} %bitcast.11), calls=%async_computation | async-start | bytes 1048576 | tf_op jit(solution)/shard_map/all_to_all | solution.py:256

commit v6 on v5

--- a/solution.py
+++ b/solution.py
@@ -13,9 +13,9 @@
 FIRST = 8
 BANDS = 4
 BAND = GRID // BANDS
-OUT_PITCH = 24
+PARTS = 2
 IN_PITCH = 17
-GROUP = 8
+GROUP = 16
 CHUNK = 16
 VMEM_BYTES = 32 * 1024 * 1024
 
@@ -70,7 +70,7 @@
 
 def channelize_kernel(frames, volt_hbm, gain_hbm, taps_hbm, twist_hbm, table_hbm, out_ref,
                       volt_ref, gain_ref, taps_ref, twist_ref, table_ref,
-                      part_ref, turn_ref, sorted_ref, sems):
+                      part_ref, turn_ref, sorted_ref, pack_ref, sems):
     sources = (volt_hbm, taps_hbm, twist_hbm, gain_hbm, table_hbm)
     targets = (volt_ref, taps_ref, twist_ref, gain_ref, table_ref)
     copies = [pltpu.make_async_copy(s, t, sems.at[i]) for i, (s, t) in enumerate(zip(sources, targets))]
@@ -109,20 +109,29 @@
     turn_ref[0:channels, 0 : 2 * antennas] = both.T
     copies[4].wait()
     blank = jnp.zeros(((2 * frames - spans) * antennas, second), jnp.float32)
-    all_spectra = jnp.dot(part_ref[...], table_ref[...], preferred_element_type=jnp.float32)
-    for k in range(FIRST):
-        spectra = all_spectra[k * spans * antennas : (k + 1) * spans * antennas]
-        gains = turn_ref[pl.ds(k, second, stride=FIRST), 0 : 2 * antennas].T
-        gain_re = jnp.concatenate([gains[0:antennas]] * spans, axis=0)
-        gain_im = jnp.concatenate([gains[antennas:]] * spans, axis=0)
-        re, im = spectra[:, 0:second], spectra[:, second:]
-        for c, volts in enumerate((re * gain_re - im * gain_im, re * gain_im + im * gain_re)):
-            turned = jnp.concatenate([volts, blank], axis=0).T
-            sorted_ref[pl.ds(2 * k + c, second, stride=OUT_PITCH), :] = turned
-    width = 2 * FIRST
-    for d in range(second):
-        out_ref[d * width : (d + 1) * width] = sorted_ref[
-            d * OUT_PITCH : d * OUT_PITCH + width].astype(jnp.bfloat16)
+    share = FIRST // PARTS
+    lines = spans * antennas
+    sends = []
+    for h in range(PARTS):
+        all_spectra = jnp.dot(
+            part_ref[h * share * lines : (h + 1) * share * lines], table_ref[...],
+            preferred_element_type=jnp.float32)
+        for q in range(share):
+            k = h * share + q
+            spectra = all_spectra[q * lines : (q + 1) * lines]
+            gains = turn_ref[pl.ds(k, second, stride=FIRST), 0 : 2 * antennas].T
+            gain_re = jnp.concatenate([gains[0:antennas]] * spans, axis=0)
+            gain_im = jnp.concatenate([gains[antennas:]] * spans, axis=0)
+            re, im = spectra[:, 0:second], spectra[:, second:]
+            for c, volts in enumerate((re * gain_re - im * gain_im, re * gain_im + im * gain_re)):
+                turned = jnp.concatenate([volts, blank], axis=0).T
+                sorted_ref[h, pl.ds(2 * q + c, second, stride=2 * share), :] = turned
+        width = 2 * share
+        pack_ref[:, h] = sorted_ref[h, 0 : second * width].reshape(second, width, second).astype(jnp.bfloat16)
+        sends.append(pltpu.make_async_copy(pack_ref.at[:, h], out_ref.at[:, h], sems.at[len(copies) + h]))
+        sends[-1].start()
+    for send in sends:
+        send.wait()
 
 
 def footprint_kernel(cells_ref, offsets_ref, right_ref, left_ref):
@@ -218,7 +227,8 @@
 
     send = pl.pallas_call(
         lambda *refs: channelize_kernel(frames, *refs),
-        out_shape=jax.ShapeDtypeStruct((rows, second), jnp.bfloat16),
+        out_shape=jax.ShapeDtypeStruct((second, PARTS, rows // second // PARTS, second), jnp.bfloat16),
+        out_specs=pl.BlockSpec(memory_space=pl.ANY),
         in_specs=[pl.BlockSpec(memory_space=pl.ANY)] * 5,
         scratch_shapes=[
             pltpu.VMEM(voltages.shape, jnp.bfloat16),
@@ -228,8 +238,9 @@
             pltpu.VMEM((2 * second, 2 * second), jnp.bfloat16),
             pltpu.VMEM((FIRST * (frames + TAPS - 1) * antennas, 2 * second), jnp.bfloat16),
             pltpu.VMEM((channels + FIRST, 128), jnp.float32),
-            pltpu.VMEM((second * OUT_PITCH + 2 * FIRST, second), jnp.float32),
-            pltpu.SemaphoreType.DMA((5,)),
+            pltpu.VMEM((PARTS, rows // PARTS + FIRST, second), jnp.float32),
+            pltpu.VMEM((second, PARTS, rows // second // PARTS, second), jnp.bfloat16),
+            pltpu.SemaphoreType.DMA((5 + PARTS,)),
         ],
         compiler_params=pltpu.CompilerParams(vmem_limit_bytes=60 * 1024 * 1024),
         name="channelize",

time: 54.7 us -> 54.7 us (level)
  no operation moved by 1% of the time
where the time goes in v6:
time: 54.7 us; the launch traced here: 54.5 us
  starting transfers between devices  22.2 us (41%)
  waiting for transfers between devices  20.3 us (37%)
  Pallas kernels  11.6 us (21%)
    all_to_all x1, starting transfers between devices, local(): lax.all_to_all(send, ('chan', 'tblk'), split_axis=0, concat_axis=0, tiled...  22.2 us
    all_to_all x1, waiting for transfers between devices, local(): lax.all_to_all(send, ('chan', 'tblk'), split_axis=0, concat_axis=0, tiled...  20.3 us
    pallas_call x1, Pallas kernels, local(): pl.pallas_call(lambda *refs: image_kernel(scale, *refs), out_shape=jax.Sh...  7.46 us
    pallas_call x1, Pallas kernels, local(): pl.pallas_call(lambda *refs: channelize_kernel(frames, *refs), out_shape=...  3.16 us
  transfers between devices with their start and end apart: 1, of which 1 were waited for; matrix products, arithmetic and copies ran while one was open for 1% of the time, Pallas kernels for 2%

profile of v6, /device:TPU:1, one launch (start us, length us, event | category | flops | bytes accessed | tf_op | source)
XLA Modules:
  0.0 54.5 jit_solution(4348102087091714710)
XLA Ops:
  0.0 0.0 copy-start
  0.0 0.0 copy-start.1
  0.0 0.0 copy-start.2
  0.0 0.0 copy-start.3
  0.0 3.2 %channelize.1 = bf16[128,2,8,128]{3,2,1,0:T(8,128)(2,1)} custom-call(bf16[2,4,16,1024]{3,2,1,0:T(8,128)(2,1)} %refs_0_.1, f32[2,16,1024]{2,1,0:T(8,128)} %refs_1_.1, f32[4,1024]{1,0:T(4,128)} %constant.8.clone.refs_2_, f32[2,8,128]{2,1,0:T(8,128)} %constant.9.clone.refs_3_, bf16[256,256]{1,0:T(8,128)(2,1)} %constant.10.clone.refs_4_.refs_3_), custom_call_target="tpu_custom_call" | custom-call | tf_op jit(solution)/shard_map/channelize/pallas_call | solution.py:228
  3.2 22.2 %all-to-all-start = ((bf16[512,4,128]{2,1,0:T(4,128)(2,1)}), bf16[512,4,128]{2,1,0:T(4,128)(2,1)S(1)}, u32[]{:S(2)}, u32[]{:S(2)}) async-start(bf16[512,4,128]{2,1,0:T(4,128)(2,1)} %bitcast.11), calls=%async_computation | async-start | bytes 1048576 | tf_op jit(solution)/shard_map/all_to_all | solution.py:267
  25.4 0.0 copy-done.2
  25.4 0.1 reshape.20
  25.5 0.1 copy.12
  25.5 0.0 copy-done.3
  25.5 0.1 reshape.22
  25.7 0.1 copy.13
  25.8 1.0 %footprint.1 = (bf16[512,2048]{1,0:T(8,128)(2,1)S(1)}, bf16[48,2048]{1,0:T(8,128)(2,1)S(1)}) custom-call(s32[2,2048]{1,0:T(2,128)S(1)} %get-tuple-element.10.cells_ref, s32[2,2048]{1,0:T(2,128)S(1)} %get-tuple-element.9.offsets_ref), custom_call_target="tpu_custom_call" | custom-call | flops 10000000 | bytes 1500000 | tf_op jit(solution)/shard_map/footprint/pallas_call | solution.py:255
  26.7 20.3 %all-to-all-done = bf16[512,4,128]{2,1,0:T(4,128)(2,1)S(1)} async-done(((bf16[512,4,128]{2,1,0:T(4,128)(2,1)}), bf16[512,4,128]{2,1,0:T(4,128)(2,1)S(1)}, u32[]{:S(2)}, u32[]{:S(2)}) %all-to-all-start) | async-done | bytes 524320 | tf_op jit(solution)/shard_map/all_to_all | solution.py:267
  47.1 0.0 copy-done
  47.1 0.0 copy-done.1
  47.1 7.5 %image.1 = f32[2,128,128]{2,1,0:T(8,128)} custom-call(bf16[2048,128]{1,0:T(8,128)(2,1)S(1)} %bitcast.10, bf16[512,2048]{1,0:T(8,128)(2,1)S(1)} %get-tuple-element.7.refs_1_, bf16[48,2048]{1,0:T(8,128)(2,1)S(1)} %get-tuple-element.8.refs_2_, bf16[256,256]{1,0:T(8,128)(2,1)S(1)} %copy-done, bf16[256,256]{1,0:T(8,128)(2,1)S(1)} %copy-done.1), custom_call_target="tpu_custom_call" | custom-call | tf_op jit(solution)/shard_map/image/pallas_call | solution.py:272
  (1 shorter events, 0.0 us)
Async XLA Ops:
  0.0 47.1 %copy-start = (bf16[256,256]{1,0:T(8,128)(2,1)S(1)}, bf16[256,256]{1,0:T(8,128)(2,1)}, u32[]{:S(2)}) copy-start(bf16[256,256]{1,0:T(8,128)(2,1)} %constant.10.clone.refs_4_.refs_3_) | copy-start | bytes 393220
  0.0 47.1 %copy-start.1 = (bf16[256,256]{1,0:T(8,128)(2,1)S(1)}, bf16[256,256]{1,0:T(8,128)(2,1)}, u32[]{:S(2)}) copy-start(bf16[256,256]{1,0:T(8,128)(2,1)} %constant.11.clone.refs_4_) | copy-start | bytes 393220
  0.0 25.4 %copy-start.2 = (s32[2,2048]{1,0:T(2,128)S(1)}, s32[2,2048]{1,0:T(2,128)}, u32[]{:S(2)}) copy-start(s32[2,2048]{1,0:T(2,128)} %param.11) | copy-start | bytes 49156
  0.0 25.5 %copy-start.3 = (s32[2,2048]{1,0:T(2,128)S(1)}, s32[2,2048]{1,0:T(2,128)}, u32[]{:S(2)}) copy-start(s32[2,2048]{1,0:T(2,128)} %param.12) | copy-start | bytes 49156
  3.2 43.9 %all-to-all-start = ((bf16[512,4,128]{2,1,0:T(4,128)(2,1)}), bf16[512,4,128]{2,1,0:T(4,128)(2,1)S(1)}, u32[]{:S(2)}, u32[]{:S(2)}) async-start(bf16[512,4,128]{2,1,0:T(4,128)(2,1)} %bitcast.11), calls=%async_computation | async-start | bytes 1048576 | tf_op jit(solution)/shard_map/all_to_all | solution.py:267

commit v7 on v6

--- a/solution.py
+++ b/solution.py
@@ -15,7 +15,7 @@
 BAND = GRID // BANDS
 PARTS = 2
 IN_PITCH = 17
-GROUP = 16
+GROUP = 8
 CHUNK = 16
 VMEM_BYTES = 32 * 1024 * 1024
 

time: 54.7 us -> 54.7 us (level)
  no operation moved by 1% of the time
where the time goes in v7:
time: 54.7 us; the launch traced here: 54.5 us
  starting transfers between devices  22.2 us (41%)
  waiting for transfers between devices  20.3 us (37%)
  Pallas kernels  11.6 us (21%)
    all_to_all x1, starting transfers between devices, local(): lax.all_to_all(send, ('chan', 'tblk'), split_axis=0, concat_axis=0, tiled...  22.2 us
    all_to_all x1, waiting for transfers between devices, local(): lax.all_to_all(send, ('chan', 'tblk'), split_axis=0, concat_axis=0, tiled...  20.3 us
    pallas_call x1, Pallas kernels, local(): pl.pallas_call(lambda *refs: image_kernel(scale, *refs), out_shape=jax.Sh...  7.46 us
    pallas_call x1, Pallas kernels, local(): pl.pallas_call(lambda *refs: channelize_kernel(frames, *refs), out_shape=...  3.16 us
  transfers between devices with their start and end apart: 1, of which 1 were waited for; matrix products, arithmetic and copies ran while one was open for 1% of the time, Pallas kernels for 2%

profile of v7, /device:TPU:1, one launch (start us, length us, event | category | flops | bytes accessed | tf_op | source)
XLA Modules:
  0.0 54.5 jit_solution(6474883255640173736)
XLA Ops:
  0.0 0.0 copy-start
  0.0 0.0 copy-start.1
  0.0 0.0 copy-start.2
  0.0 0.0 copy-start.3
  0.0 3.2 %channelize.1 = bf16[128,2,8,128]{3,2,1,0:T(8,128)(2,1)} custom-call(bf16[2,4,16,1024]{3,2,1,0:T(8,128)(2,1)} %refs_0_.1, f32[2,16,1024]{2,1,0:T(8,128)} %refs_1_.1, f32[4,1024]{1,0:T(4,128)} %constant.8.clone.refs_2_, f32[2,8,128]{2,1,0:T(8,128)} %constant.9.clone.refs_3_, bf16[256,256]{1,0:T(8,128)(2,1)} %constant.10.clone.refs_4_.refs_3_), custom_call_target="tpu_custom_call" | custom-call | tf_op jit(solution)/shard_map/channelize/pallas_call | solution.py:228
  3.2 22.2 %all-to-all-start = ((bf16[512,4,128]{2,1,0:T(4,128)(2,1)}), bf16[512,4,128]{2,1,0:T(4,128)(2,1)S(1)}, u32[]{:S(2)}, u32[]{:S(2)}) async-start(bf16[512,4,128]{2,1,0:T(4,128)(2,1)} %bitcast.11), calls=%async_computation | async-start | bytes 1048576 | tf_op jit(solution)/shard_map/all_to_all | solution.py:267
  25.4 0.0 copy-done.2
  25.4 0.1 reshape.20
  25.5 0.1 copy.12
  25.5 0.0 copy-done.3
  25.5 0.1 reshape.22
  25.7 0.1 copy.13
  25.8 1.0 %footprint.1 = (bf16[512,2048]{1,0:T(8,128)(2,1)S(1)}, bf16[48,2048]{1,0:T(8,128)(2,1)S(1)}) custom-call(s32[2,2048]{1,0:T(2,128)S(1)} %get-tuple-element.10.cells_ref, s32[2,2048]{1,0:T(2,128)S(1)} %get-tuple-element.9.offsets_ref), custom_call_target="tpu_custom_call" | custom-call | flops 10000000 | bytes 1500000 | tf_op jit(solution)/shard_map/footprint/pallas_call | solution.py:255
  26.7 20.3 %all-to-all-done = bf16[512,4,128]{2,1,0:T(4,128)(2,1)S(1)} async-done(((bf16[512,4,128]{2,1,0:T(4,128)(2,1)}), bf16[512,4,128]{2,1,0:T(4,128)(2,1)S(1)}, u32[]{:S(2)}, u32[]{:S(2)}) %all-to-all-start) | async-done | bytes 524320 | tf_op jit(solution)/shard_map/all_to_all | solution.py:267
  47.1 0.0 copy-done
  47.1 0.0 copy-done.1
  47.1 7.5 %image.1 = f32[2,128,128]{2,1,0:T(8,128)} custom-call(bf16[2048,128]{1,0:T(8,128)(2,1)S(1)} %bitcast.10, bf16[512,2048]{1,0:T(8,128)(2,1)S(1)} %get-tuple-element.7.refs_1_, bf16[48,2048]{1,0:T(8,128)(2,1)S(1)} %get-tuple-element.8.refs_2_, bf16[256,256]{1,0:T(8,128)(2,1)S(1)} %copy-done, bf16[256,256]{1,0:T(8,128)(2,1)S(1)} %copy-done.1), custom_call_target="tpu_custom_call" | custom-call | tf_op jit(solution)/shard_map/image/pallas_call | solution.py:272
  (1 shorter events, 0.0 us)
Async XLA Ops:
  0.0 47.1 %copy-start = (bf16[256,256]{1,0:T(8,128)(2,1)S(1)}, bf16[256,256]{1,0:T(8,128)(2,1)}, u32[]{:S(2)}) copy-start(bf16[256,256]{1,0:T(8,128)(2,1)} %constant.10.clone.refs_4_.refs_3_) | copy-start | bytes 393220
  0.0 47.1 %copy-start.1 = (bf16[256,256]{1,0:T(8,128)(2,1)S(1)}, bf16[256,256]{1,0:T(8,128)(2,1)}, u32[]{:S(2)}) copy-start(bf16[256,256]{1,0:T(8,128)(2,1)} %constant.11.clone.refs_4_) | copy-start | bytes 393220
  0.0 25.4 %copy-start.2 = (s32[2,2048]{1,0:T(2,128)S(1)}, s32[2,2048]{1,0:T(2,128)}, u32[]{:S(2)}) copy-start(s32[2,2048]{1,0:T(2,128)} %param.11) | copy-start | bytes 49156
  0.0 25.5 %copy-start.3 = (s32[2,2048]{1,0:T(2,128)S(1)}, s32[2,2048]{1,0:T(2,128)}, u32[]{:S(2)}) copy-start(s32[2,2048]{1,0:T(2,128)} %param.12) | copy-start | bytes 49156
  3.2 43.9 %all-to-all-start = ((bf16[512,4,128]{2,1,0:T(4,128)(2,1)}), bf16[512,4,128]{2,1,0:T(4,128)(2,1)S(1)}, u32[]{:S(2)}, u32[]{:S(2)}) async-start(bf16[512,4,128]{2,1,0:T(4,128)(2,1)} %bitcast.11), calls=%async_computation | async-start | bytes 1048576 | tf_op jit(solution)/shard_map/all_to_all | solution.py:267

commit v8 on v7

--- a/solution.py
+++ b/solution.py
@@ -152,7 +152,7 @@
 
 
 def image_kernel(scale, x_ref, right_ref, left_ref, first_ref, second_ref, out_ref,
-                 wide_ref, volt_ref, spread_ref, grid_ref, side_ref):
+                 wide_ref, volt_ref, spread_ref, grid_ref, side_ref, sky_ref, sems):
     blocks = 4
     frames = 4
     antennas = 16
@@ -199,6 +199,7 @@
         return carry
 
     lax.fori_loop(0, 2 * blocks * frames // CHUNK, chunk, 0)
+    sends = []
     for kk in range(2):
         total = None
         for t in range(0, blocks * frames, GROUP):
@@ -214,7 +215,11 @@
             for f in range(GROUP):
                 part = power[:, f * GRID : (f + 1) * GRID]
                 total = part if total is None else total + part
-        out_ref[kk] = total * scale
+        sky_ref[kk] = total * scale
+        sends.append(pltpu.make_async_copy(sky_ref.at[kk], out_ref.at[kk], sems.at[kk]))
+        sends[-1].start()
+    for send in sends:
+        send.wait()
 
 
 def local(voltages, calibrated_gain, cells, offsets):
@@ -272,12 +277,15 @@
     return pl.pallas_call(
         lambda *refs: image_kernel(scale, *refs),
         out_shape=jax.ShapeDtypeStruct((2, GRID, GRID), jnp.float32),
+        out_specs=pl.BlockSpec(memory_space=pl.ANY),
         scratch_shapes=[
             pltpu.VMEM((128 * IN_PITCH + 16, second), jnp.float32),
             pltpu.VMEM((chunks, members, antennas, 128), jnp.float32),
             pltpu.VMEM((members * (BAND + 1), all_antennas), jnp.bfloat16),
             pltpu.VMEM((members * (BAND + 1), BANDS * GRID), jnp.float32),
             pltpu.VMEM((chunks * CHUNK, GRID, 2 * GRID), jnp.bfloat16),
+            pltpu.VMEM((2, GRID, GRID), jnp.float32),
+            pltpu.SemaphoreType.DMA((2,)),
         ],
         compiler_params=pltpu.CompilerParams(vmem_limit_bytes=VMEM_BYTES),
         name="image",

time: 54.7 us -> 54.7 us (level)
  no operation moved by 1% of the time
where the time goes in v8:
time: 54.7 us; the launch traced here: 54.5 us
  starting transfers between devices  22.2 us (41%)
  waiting for transfers between devices  20.3 us (37%)
  Pallas kernels  11.6 us (21%)
    all_to_all x1, starting transfers between devices, local(): lax.all_to_all(send, ('chan', 'tblk'), split_axis=0, concat_axis=0, tiled...  22.2 us
    all_to_all x1, waiting for transfers between devices, local(): lax.all_to_all(send, ('chan', 'tblk'), split_axis=0, concat_axis=0, tiled...  20.3 us
    pallas_call x1, Pallas kernels, local(): pl.pallas_call(lambda *refs: image_kernel(scale, *refs), out_shape=jax.Sh...  7.45 us
    pallas_call x1, Pallas kernels, local(): pl.pallas_call(lambda *refs: channelize_kernel(frames, *refs), out_shape=...  3.16 us
  transfers between devices with their start and end apart: 1, of which 1 were waited for; matrix products, arithmetic and copies ran while one was open for 1% of the time, Pallas kernels for 2%

profile of v8, /device:TPU:1, one launch (start us, length us, event | category | flops | bytes accessed | tf_op | source)
XLA Modules:
  0.0 54.5 jit_solution(4068887960629054499)
XLA Ops:
  0.0 0.0 copy-start
  0.0 0.0 copy-start.1
  0.0 0.0 copy-start.2
  0.0 0.0 copy-start.3
  0.0 3.2 %channelize.1 = bf16[128,2,8,128]{3,2,1,0:T(8,128)(2,1)} custom-call(bf16[2,4,16,1024]{3,2,1,0:T(8,128)(2,1)} %refs_0_.1, f32[2,16,1024]{2,1,0:T(8,128)} %refs_1_.1, f32[4,1024]{1,0:T(4,128)} %constant.8.clone.refs_2_, f32[2,8,128]{2,1,0:T(8,128)} %constant.9.clone.refs_3_, bf16[256,256]{1,0:T(8,128)(2,1)} %constant.10.clone.refs_4_.refs_3_), custom_call_target="tpu_custom_call" | custom-call | tf_op jit(solution)/shard_map/channelize/pallas_call | solution.py:233
  3.2 22.2 %all-to-all-start = ((bf16[512,4,128]{2,1,0:T(4,128)(2,1)}), bf16[512,4,128]{2,1,0:T(4,128)(2,1)S(1)}, u32[]{:S(2)}, u32[]{:S(2)}) async-start(bf16[512,4,128]{2,1,0:T(4,128)(2,1)} %bitcast.11), calls=%async_computation | async-start | bytes 1048576 | tf_op jit(solution)/shard_map/all_to_all | solution.py:272
  25.4 0.0 copy-done.2
  25.4 0.1 reshape.20
  25.5 0.1 copy.12
  25.5 0.0 copy-done.3
  25.5 0.1 reshape.22
  25.7 0.1 copy.13
  25.8 1.0 %footprint.1 = (bf16[512,2048]{1,0:T(8,128)(2,1)S(1)}, bf16[48,2048]{1,0:T(8,128)(2,1)S(1)}) custom-call(s32[2,2048]{1,0:T(2,128)S(1)} %get-tuple-element.10.cells_ref, s32[2,2048]{1,0:T(2,128)S(1)} %get-tuple-element.9.offsets_ref), custom_call_target="tpu_custom_call" | custom-call | flops 10000000 | bytes 1500000 | tf_op jit(solution)/shard_map/footprint/pallas_call | solution.py:260
  26.7 20.3 %all-to-all-done = bf16[512,4,128]{2,1,0:T(4,128)(2,1)S(1)} async-done(((bf16[512,4,128]{2,1,0:T(4,128)(2,1)}), bf16[512,4,128]{2,1,0:T(4,128)(2,1)S(1)}, u32[]{:S(2)}, u32[]{:S(2)}) %all-to-all-start) | async-done | bytes 524320 | tf_op jit(solution)/shard_map/all_to_all | solution.py:272
  47.1 0.0 copy-done
  47.1 0.0 copy-done.1
  47.1 7.5 %image.1 = f32[2,128,128]{2,1,0:T(8,128)} custom-call(bf16[2048,128]{1,0:T(8,128)(2,1)S(1)} %bitcast.10, bf16[512,2048]{1,0:T(8,128)(2,1)S(1)} %get-tuple-element.7.refs_1_, bf16[48,2048]{1,0:T(8,128)(2,1)S(1)} %get-tuple-element.8.refs_2_, bf16[256,256]{1,0:T(8,128)(2,1)S(1)} %copy-done, bf16[256,256]{1,0:T(8,128)(2,1)S(1)} %copy-done.1), custom_call_target="tpu_custom_call" | custom-call | tf_op jit(solution)/shard_map/image/pallas_call | solution.py:277
  (1 shorter events, 0.0 us)
Async XLA Ops:
  0.0 47.1 %copy-start = (bf16[256,256]{1,0:T(8,128)(2,1)S(1)}, bf16[256,256]{1,0:T(8,128)(2,1)}, u32[]{:S(2)}) copy-start(bf16[256,256]{1,0:T(8,128)(2,1)} %constant.10.clone.refs_4_.refs_3_) | copy-start | bytes 393220
  0.0 47.1 %copy-start.1 = (bf16[256,256]{1,0:T(8,128)(2,1)S(1)}, bf16[256,256]{1,0:T(8,128)(2,1)}, u32[]{:S(2)}) copy-start(bf16[256,256]{1,0:T(8,128)(2,1)} %constant.11.clone.refs_4_) | copy-start | bytes 393220
  0.0 25.4 %copy-start.2 = (s32[2,2048]{1,0:T(2,128)S(1)}, s32[2,2048]{1,0:T(2,128)}, u32[]{:S(2)}) copy-start(s32[2,2048]{1,0:T(2,128)} %param.11) | copy-start | bytes 49156
  0.0 25.5 %copy-start.3 = (s32[2,2048]{1,0:T(2,128)S(1)}, s32[2,2048]{1,0:T(2,128)}, u32[]{:S(2)}) copy-start(s32[2,2048]{1,0:T(2,128)} %param.12) | copy-start | bytes 49156
  3.2 43.9 %all-to-all-start = ((bf16[512,4,128]{2,1,0:T(4,128)(2,1)}), bf16[512,4,128]{2,1,0:T(4,128)(2,1)S(1)}, u32[]{:S(2)}, u32[]{:S(2)}) async-start(bf16[512,4,128]{2,1,0:T(4,128)(2,1)} %bitcast.11), calls=%async_computation | async-start | bytes 1048576 | tf_op jit(solution)/shard_map/all_to_all | solution.py:272

commit v9 on v7

--- a/solution.py
+++ b/solution.py
@@ -15,7 +15,7 @@
 BAND = GRID // BANDS
 PARTS = 2
 IN_PITCH = 17
-GROUP = 8
+GROUP = 4
 CHUNK = 16
 VMEM_BYTES = 32 * 1024 * 1024
 

time: 54.7 us -> 54.7 us (level)
  no operation moved by 1% of the time
where the time goes in v9:
time: 54.7 us; the launch traced here: 54.5 us
  starting transfers between devices  22.2 us (41%)
  waiting for transfers between devices  20.3 us (37%)
  Pallas kernels  11.6 us (21%)
    all_to_all x1, starting transfers between devices, local(): lax.all_to_all(send, ('chan', 'tblk'), split_axis=0, concat_axis=0, tiled...  22.2 us
    all_to_all x1, waiting for transfers between devices, local(): lax.all_to_all(send, ('chan', 'tblk'), split_axis=0, concat_axis=0, tiled...  20.3 us
    pallas_call x1, Pallas kernels, local(): pl.pallas_call(lambda *refs: image_kernel(scale, *refs), out_shape=jax.Sh...  7.46 us
    pallas_call x1, Pallas kernels, local(): pl.pallas_call(lambda *refs: channelize_kernel(frames, *refs), out_shape=...  3.16 us
  transfers between devices with their start and end apart: 1, of which 1 were waited for; matrix products, arithmetic and copies ran while one was open for 1% of the time, Pallas kernels for 2%

profile of v9, /device:TPU:1, one launch (start us, length us, event | category | flops | bytes accessed | tf_op | source)
XLA Modules:
  0.0 54.5 jit_solution(12410553775422975918)
XLA Ops:
  0.0 0.0 copy-start
  0.0 0.0 copy-start.1
  0.0 0.0 copy-start.2
  0.0 0.0 copy-start.3
  0.0 3.2 %channelize.1 = bf16[128,2,8,128]{3,2,1,0:T(8,128)(2,1)} custom-call(bf16[2,4,16,1024]{3,2,1,0:T(8,128)(2,1)} %refs_0_.1, f32[2,16,1024]{2,1,0:T(8,128)} %refs_1_.1, f32[4,1024]{1,0:T(4,128)} %constant.8.clone.refs_2_, f32[2,8,128]{2,1,0:T(8,128)} %constant.9.clone.refs_3_, bf16[256,256]{1,0:T(8,128)(2,1)} %constant.10.clone.refs_4_.refs_3_), custom_call_target="tpu_custom_call" | custom-call | tf_op jit(solution)/shard_map/channelize/pallas_call | solution.py:228
  3.2 22.2 %all-to-all-start = ((bf16[512,4,128]{2,1,0:T(4,128)(2,1)}), bf16[512,4,128]{2,1,0:T(4,128)(2,1)S(1)}, u32[]{:S(2)}, u32[]{:S(2)}) async-start(bf16[512,4,128]{2,1,0:T(4,128)(2,1)} %bitcast.11), calls=%async_computation | async-start | bytes 1048576 | tf_op jit(solution)/shard_map/all_to_all | solution.py:267
  25.4 0.0 copy-done.2
  25.4 0.1 reshape.20
  25.5 0.1 copy.12
  25.5 0.0 copy-done.3
  25.5 0.1 reshape.22
  25.7 0.1 copy.13
  25.8 1.0 %footprint.1 = (bf16[512,2048]{1,0:T(8,128)(2,1)S(1)}, bf16[48,2048]{1,0:T(8,128)(2,1)S(1)}) custom-call(s32[2,2048]{1,0:T(2,128)S(1)} %get-tuple-element.10.cells_ref, s32[2,2048]{1,0:T(2,128)S(1)} %get-tuple-element.9.offsets_ref), custom_call_target="tpu_custom_call" | custom-call | flops 10000000 | bytes 1500000 | tf_op jit(solution)/shard_map/footprint/pallas_call | solution.py:255
  26.7 20.3 %all-to-all-done = bf16[512,4,128]{2,1,0:T(4,128)(2,1)S(1)} async-done(((bf16[512,4,128]{2,1,0:T(4,128)(2,1)}), bf16[512,4,128]{2,1,0:T(4,128)(2,1)S(1)}, u32[]{:S(2)}, u32[]{:S(2)}) %all-to-all-start) | async-done | bytes 524320 | tf_op jit(solution)/shard_map/all_to_all | solution.py:267
  47.1 0.0 copy-done
  47.1 0.0 copy-done.1
  47.1 7.5 %image.1 = f32[2,128,128]{2,1,0:T(8,128)} custom-call(bf16[2048,128]{1,0:T(8,128)(2,1)S(1)} %bitcast.10, bf16[512,2048]{1,0:T(8,128)(2,1)S(1)} %get-tuple-element.7.refs_1_, bf16[48,2048]{1,0:T(8,128)(2,1)S(1)} %get-tuple-element.8.refs_2_, bf16[256,256]{1,0:T(8,128)(2,1)S(1)} %copy-done, bf16[256,256]{1,0:T(8,128)(2,1)S(1)} %copy-done.1), custom_call_target="tpu_custom_call" | custom-call | tf_op jit(solution)/shard_map/image/pallas_call | solution.py:272
  (1 shorter events, 0.0 us)
Async XLA Ops:
  0.0 47.1 %copy-start = (bf16[256,256]{1,0:T(8,128)(2,1)S(1)}, bf16[256,256]{1,0:T(8,128)(2,1)}, u32[]{:S(2)}) copy-start(bf16[256,256]{1,0:T(8,128)(2,1)} %constant.10.clone.refs_4_.refs_3_) | copy-start | bytes 393220
  0.0 47.1 %copy-start.1 = (bf16[256,256]{1,0:T(8,128)(2,1)S(1)}, bf16[256,256]{1,0:T(8,128)(2,1)}, u32[]{:S(2)}) copy-start(bf16[256,256]{1,0:T(8,128)(2,1)} %constant.11.clone.refs_4_) | copy-start | bytes 393220
  0.0 25.4 %copy-start.2 = (s32[2,2048]{1,0:T(2,128)S(1)}, s32[2,2048]{1,0:T(2,128)}, u32[]{:S(2)}) copy-start(s32[2,2048]{1,0:T(2,128)} %param.11) | copy-start | bytes 49156
  0.0 25.5 %copy-start.3 = (s32[2,2048]{1,0:T(2,128)S(1)}, s32[2,2048]{1,0:T(2,128)}, u32[]{:S(2)}) copy-start(s32[2,2048]{1,0:T(2,128)} %param.12) | copy-start | bytes 49156
  3.2 43.9 %all-to-all-start = ((bf16[512,4,128]{2,1,0:T(4,128)(2,1)}), bf16[512,4,128]{2,1,0:T(4,128)(2,1)S(1)}, u32[]{:S(2)}, u32[]{:S(2)}) async-start(bf16[512,4,128]{2,1,0:T(4,128)(2,1)} %bitcast.11), calls=%async_computation | async-start | bytes 1048576 | tf_op jit(solution)/shard_map/all_to_all | solution.py:267
